TPU v7x, 256 devices: a whole 4x4x8 slice. The times are simulated.
256 devices in a mesh: row: 8 (over y, core), col: 8 (over z), level: 4 (over x).
Axes of the slice: x: 4, y: 4, z: 8, core: 2. Of those that a mesh axis runs over, the one named last changes fastest.
Arguments:
- pre_acts: bfloat16 [4, 2, 512, 64, 1024], P('level', None, 'row', None, 'col'), may hold values from -6 to 6
- pred_cot: bfloat16 [4, 512, 1024], P('level', 'row', 'col'), may hold values from -6 to 6
- occupancy: int32 [4, 512, 1024], P('level', 'row', 'col'), may hold values from 0 to 1
- conv_weights: bfloat16 [4, 2, 3, 3, 64, 64], P('level'), may hold values from -0.25 to 0.25
- coupling: bfloat16 [4, 2, 64], P('level'), may hold values from -3 to 3
- dilation: int32 [2], replicated, may hold values from 1 to 16, as said below
Outputs:
- attribution: bfloat16 [4, 512, 64, 1024], P('level', 'row', None, 'col')
Inputs may be any that keep to these rules, and one draw needn't show every extreme that they name: Some layer has dilation 16.
All inputs are finite; a program needn't handle non-finite values.
Results may differ from a plain program's by a relative error of at most 0.02.
Values may be sent and summed in bfloat16 or wider, within the bound.
A program may use at most 64 MiB of HBM per device.

v0:
```python
import jax
import jax.numpy as jnp
from jax import lax
from jax.sharding import PartitionSpec as P

DMAX = 16


def extended(block, sides, width):
    for axis, dim in sides:
        count = lax.axis_size(axis)
        forward = [(i, i + 1) for i in range(count - 1)]
        backward = [(target, source) for source, target in forward]
        low = lax.ppermute(
            lax.slice_in_dim(block, block.shape[dim] - width, None, axis=dim), axis, forward
        )
        high = lax.ppermute(lax.slice_in_dim(block, 0, width, axis=dim), axis, backward)
        block = jnp.concatenate([low, block, high], axis=dim)
    return block


def shifted(value, axis, steps):
    count = lax.axis_size(axis)
    first, last = (max(0, -steps), min(count, count - steps))
    return lax.ppermute(value, axis, [(source, source + steps) for source in range(first, last)])


def backprop(layer_weights, head_row, pre_level, cot_level, incoming, dilation, extend):
    total = cot_level.astype(jnp.float32) + incoming
    gradient = head_row.astype(jnp.float32)[None, :, None] * total[:, None, :]
    rows_here = gradient.shape[0]
    channels = gradient.shape[1]
    cols_here = gradient.shape[2]
    zero_index = jnp.zeros((), jnp.int32)
    for layer in reversed(range(pre_level.shape[0])):
        masked = jnp.where(pre_level[layer] > 0, gradient, 0.0).astype(jnp.bfloat16)
        padded = extend(masked)
        spacing = dilation[layer]
        pieces = []
        for a in (-1, 0, 1):
            for b in (-1, 0, 1):
                start_row = DMAX - a * spacing
                start_col = DMAX - b * spacing
                pieces.append(
                    lax.dynamic_slice(
                        padded, (start_row, zero_index, start_col), (rows_here, channels, cols_here)
                    )
                )
        stacked = jnp.stack(pieces)
        kernels = layer_weights[layer].reshape(9, channels, channels)
        gradient = gradient + jnp.einsum(
            "toc,trow->rcw", kernels, stacked, preferred_element_type=jnp.float32
        )
    return gradient


def contract(entry_row, gradient):
    return jnp.sum(entry_row.astype(jnp.float32)[None, :, None] * gradient, axis=1)


def on_device(pre_acts, pred_cot, occupancy, conv_weights, coupling, dilation):
    start_cot = jnp.where(occupancy > 0, pred_cot, jnp.zeros_like(pred_cot))

    def with_rim(masked):
        return extended(masked, (("row", 0), ("col", 2)), DMAX)

    levels = lax.axis_size("level")
    incoming = jnp.zeros((start_cot.shape[1], start_cot.shape[2]), jnp.float32)
    gradient = None
    for hop_index in range(levels):
        gradient = backprop(
            conv_weights[0], coupling[0, 0], pre_acts[0], start_cot[0], incoming, dilation, with_rim
        )
        if hop_index + 1 < levels:
            outgoing = contract(coupling[0, 1], gradient)
            incoming = shifted(outgoing.astype(jnp.bfloat16), "level", -1).astype(outgoing.dtype)
    return gradient.astype(jnp.bfloat16)[None]


def solution(mesh):
    return jax.shard_map(
        on_device,
        mesh=mesh,
        in_specs=(
            P("level", None, "row", None, "col"),
            P("level", "row", "col"),
            P("level", "row", "col"),
            P("level", None, None, None, None, None),
            P("level", None, None),
            P(),
        ),
        out_specs=P("level", "row", None, "col"),
        check_vma=False,
    )
```

profile of v0, /device:TPU:1, one launch (start us, length us, event | category | flops | bytes accessed | tf_op | source)
XLA Modules:
  0.0 414.5 jit_solution(15262053682862295097)
XLA Ops:
  3.4 4.6 %collective-permute-start = (bf16[16,64,128]{2,1,0:T(8,128)(2,1)S(1)}, bf16[16,64,128]{2,1,0:T(8,128)(2,1)S(1)}, u32[]{:S(2)}, u32[]{:S(2)}) collective-permute-start(bf16[16,64,128]{2,1,0:T(8,128)(2,1)S(1)} %get-tuple-element.41), channel_id=1, source_target_pairs={{0,32},{32,64},{64,96},{96,128},{128,160},{160,192},{192,224},{1,3... | collective-permute-start | bytes 786440 | tf_op jit(solution)/shard_map/ppermute | solution.py:14
  25.3 5.0 %collective-permute-start.2 = (bf16[96,64,16]{0,2,1:T(8,128)(2,1)}, bf16[96,64,16]{0,2,1:T(8,128)(2,1)}, u32[]{:S(2)}, u32[]{:S(2)}) collective-permute-start(bf16[96,64,16]{0,2,1:T(8,128)(2,1)} %copy.13), channel_id=1, source_target_pairs={{0,4},{4,8},{8,12},{12,16},{16,20},{20,24},{24,28},{1,5},{5,9},{9,... | collective-permute-start | bytes 589832 | tf_op jit(solution)/shard_map/ppermute | solution.py:14
  37.1 4.0 copy.16
  41.0 3.9 pad_maximum_fusion
  54.7 4.0 collective-permute-start.4
  62.0 4.4 %collective-permute-done.5 = bf16[16,64,128]{2,1,0:T(8,128)(2,1)S(1)} collective-permute-done((bf16[16,64,128]{2,1,0:T(8,128)(2,1)S(1)}, bf16[16,64,128]{2,1,0:T(8,128)(2,1)S(1)}, u32[]{:S(2)}, u32[]{:S(2)}) %collective-permute-start.5) | collective-permute-done | bytes 262176 | tf_op jit(solution)/shard_map/ppermute | solution.py:17
  71.6 4.5 %collective-permute-start.6 = (bf16[96,64,16]{0,2,1:T(8,128)(2,1)S(1)}, bf16[96,64,16]{0,2,1:T(8,128)(2,1)S(1)}, u32[]{:S(2)}, u32[]{:S(2)}) collective-permute-start(bf16[96,64,16]{0,2,1:T(8,128)(2,1)S(1)} %copy.18), channel_id=1, source_target_pairs={{0,4},{4,8},{8,12},{12,16},{16,20},{20,24},{24,28},{1,5},{5,9},{9,... | collective-permute-start | bytes 589832 | tf_op jit(solution)/shard_map/ppermute | solution.py:14
  87.0 3.9 copy.21
  91.0 4.1 pad_maximum_fusion.1
  107.9 6.0 %collective-permute-start.9 = (bf16[16,64,128]{2,1,0:T(8,128)(2,1)S(1)}, bf16[16,64,128]{2,1,0:T(8,128)(2,1)S(1)}, u32[]{:S(2)}, u32[]{:S(2)}) collective-permute-start(bf16[16,64,128]{2,1,0:T(8,128)(2,1)S(1)} %get-tuple-element.37), channel_id=1, source_target_pairs={{0,32},{32,64},{64,96},{96,128},{128,160},{160,192},{192,224},{1,3... | collective-permute-start | bytes 786440 | tf_op jit(solution)/shard_map/ppermute | solution.py:14
  117.2 4.4 %collective-permute-done.10 = bf16[16,64,128]{2,1,0:T(8,128)(2,1)S(1)} collective-permute-done((bf16[16,64,128]{2,1,0:T(8,128)(2,1)S(1)}, bf16[16,64,128]{2,1,0:T(8,128)(2,1)S(1)}, u32[]{:S(2)}, u32[]{:S(2)}) %collective-permute-start.10) | collective-permute-done | bytes 262176 | tf_op jit(solution)/shard_map/ppermute | solution.py:17
  126.8 4.6 %collective-permute-start.11 = (bf16[96,64,16]{0,2,1:T(8,128)(2,1)S(1)}, bf16[96,64,16]{0,2,1:T(8,128)(2,1)}, u32[]{:S(2)}, u32[]{:S(2)}) collective-permute-start(bf16[96,64,16]{0,2,1:T(8,128)(2,1)S(1)} %copy.24), channel_id=1, source_target_pairs={{0,4},{4,8},{8,12},{12,16},{16,20},{20,24},{24,28},{1,5},{5,9},{9,... | collective-permute-start | bytes 589832 | tf_op jit(solution)/shard_map/ppermute | solution.py:14
  136.1 4.0 copy.26
  147.3 4.1 pad_maximum_fusion.2
  168.1 4.4 %collective-permute-done.14 = bf16[16,64,128]{2,1,0:T(8,128)(2,1)S(1)} collective-permute-done((bf16[16,64,128]{2,1,0:T(8,128)(2,1)S(1)}, bf16[16,64,128]{2,1,0:T(8,128)(2,1)S(1)}, u32[]{:S(2)}, u32[]{:S(2)}) %collective-permute-start.14) | collective-permute-done | bytes 262176 | tf_op jit(solution)/shard_map/ppermute | solution.py:17
  177.7 6.7 %collective-permute-start.15 = (bf16[96,64,16]{0,2,1:T(8,128)(2,1)S(1)}, bf16[96,64,16]{0,2,1:T(8,128)(2,1)}, u32[]{:S(2)}, u32[]{:S(2)}) collective-permute-start(bf16[96,64,16]{0,2,1:T(8,128)(2,1)S(1)} %copy.28), channel_id=1, source_target_pairs={{0,4},{4,8},{8,12},{12,16},{16,20},{20,24},{24,28},{1,5},{5,9},{9,... | collective-permute-start | bytes 589832 | tf_op jit(solution)/shard_map/ppermute | solution.py:14
  195.2 3.9 copy.31
  199.1 4.1 pad_maximum_fusion.3
  216.0 7.1 %collective-permute-start.18 = (bf16[16,64,128]{2,1,0:T(8,128)(2,1)S(1)}, bf16[16,64,128]{2,1,0:T(8,128)(2,1)S(1)}, u32[]{:S(2)}, u32[]{:S(2)}) collective-permute-start(bf16[16,64,128]{2,1,0:T(8,128)(2,1)S(1)} %get-tuple-element.33), channel_id=1, source_target_pairs={{0,32},{32,64},{64,96},{96,128},{128,160},{160,192},{192,224},{1,3... | collective-permute-start | bytes 786440 | tf_op jit(solution)/shard_map/ppermute | solution.py:14
  226.4 4.4 %collective-permute-done.19 = bf16[16,64,128]{2,1,0:T(8,128)(2,1)S(1)} collective-permute-done((bf16[16,64,128]{2,1,0:T(8,128)(2,1)S(1)}, bf16[16,64,128]{2,1,0:T(8,128)(2,1)S(1)}, u32[]{:S(2)}, u32[]{:S(2)}) %collective-permute-start.19) | collective-permute-done | bytes 262176 | tf_op jit(solution)/shard_map/ppermute | solution.py:17
  253.7 4.1 pad_maximum_fusion.4
  274.3 4.4 %collective-permute-done.23 = bf16[16,64,128]{2,1,0:T(8,128)(2,1)S(1)} collective-permute-done((bf16[16,64,128]{2,1,0:T(8,128)(2,1)S(1)}, bf16[16,64,128]{2,1,0:T(8,128)(2,1)S(1)}, u32[]{:S(2)}, u32[]{:S(2)}) %collective-permute-start.23) | collective-permute-done | bytes 262176 | tf_op jit(solution)/shard_map/ppermute | solution.py:17
  284.6 4.0 collective-permute-start.24
  302.2 3.9 pad_maximum_fusion.5
  318.9 4.3 %collective-permute-start.27 = (bf16[16,64,128]{2,1,0:T(8,128)(2,1)S(1)}, bf16[16,64,128]{2,1,0:T(8,128)(2,1)S(1)}, u32[]{:S(2)}, u32[]{:S(2)}) collective-permute-start(bf16[16,64,128]{2,1,0:T(8,128)(2,1)S(1)} %get-tuple-element.29), channel_id=1, source_target_pairs={{0,32},{32,64},{64,96},{96,128},{128,160},{160,192},{192,224},{1,3... | collective-permute-start | bytes 786440 | tf_op jit(solution)/shard_map/ppermute | solution.py:14
  326.5 4.4 %collective-permute-done.28 = bf16[16,64,128]{2,1,0:T(8,128)(2,1)S(1)} collective-permute-done((bf16[16,64,128]{2,1,0:T(8,128)(2,1)S(1)}, bf16[16,64,128]{2,1,0:T(8,128)(2,1)S(1)}, u32[]{:S(2)}, u32[]{:S(2)}) %collective-permute-start.28) | collective-permute-done | bytes 262176 | tf_op jit(solution)/shard_map/ppermute | solution.py:17
  349.7 3.9 copy.45
  353.7 3.9 pad_maximum_fusion.6
  372.4 4.4 %collective-permute-done.32 = bf16[16,64,128]{2,1,0:T(8,128)(2,1)S(1)} collective-permute-done((bf16[16,64,128]{2,1,0:T(8,128)(2,1)S(1)}, bf16[16,64,128]{2,1,0:T(8,128)(2,1)S(1)}, u32[]{:S(2)}, u32[]{:S(2)}) %collective-permute-start.32) | collective-permute-done | bytes 262176 | tf_op jit(solution)/shard_map/ppermute | solution.py:17
  391.2 4.0 copy.48
  397.3 3.9 copy.49
  401.2 4.2 %pad_maximum_fusion.7 = bf16[96,64,160]{2,1,0:T(8,128)(2,1)S(1)} fusion(bf16[96,64,16]{2,1,0:T(8,128)(2,1)} %copy.49, bf16[16,64,128]{2,1,0:T(8,128)(2,1)} %copy-done.13, bf16[64,64,128]{2,1,0:T(8,128)(2,1)S(1)} %get-tuple-element.54, bf16[16,64,128]{2,1,0:T(8,128)(2,1)} %copy-done.10, bf16[96,64,16]{2,1,0:T(8,128)(2,1)} %copy.48), kind=kLoop, calls=%fused_computation.7 | loop fusion | flops 9830400 | bytes 3932160 | tf_op jit(solution)/shard_map/concatenate | solution.py:18
  (223 shorter events, 266.1 us)
Async XLA Ops:
  3.4 9.7 %collective-permute-start = (bf16[16,64,128]{2,1,0:T(8,128)(2,1)S(1)}, bf16[16,64,128]{2,1,0:T(8,128)(2,1)S(1)}, u32[]{:S(2)}, u32[]{:S(2)}) collective-permute-start(bf16[16,64,128]{2,1,0:T(8,128)(2,1)S(1)} %get-tuple-element.41), channel_id=1, source_target_pairs={{0,32},{32,64},{64,96},{96,128},{128,160},{160,192},{192,224},{1,3... | collective-permute-start | bytes 786440 | tf_op jit(solution)/shard_map/ppermute | solution.py:14
  8.0 7.7 %collective-permute-start.1 = (bf16[16,64,128]{2,1,0:T(8,128)(2,1)S(1)}, bf16[16,64,128]{2,1,0:T(8,128)(2,1)S(1)}, u32[]{:S(2)}, u32[]{:S(2)}) collective-permute-start(bf16[16,64,128]{2,1,0:T(8,128)(2,1)S(1)} %get-tuple-element.42), channel_id=1, source_target_pairs={{32,0},{64,32},{96,64},{128,96},{160,128},{192,160},{224,192},{33,... | collective-permute-start | bytes 786440 | tf_op jit(solution)/shard_map/ppermute | solution.py:17
  24.0 13.1 %collective-permute-start.3 = (bf16[96,64,16]{0,2,1:T(8,128)(2,1)}, bf16[96,64,16]{0,2,1:T(8,128)(2,1)}, u32[]{:S(2)}, u32[]{:S(2)}) collective-permute-start(bf16[96,64,16]{0,2,1:T(8,128)(2,1)} %copy.14), channel_id=1, source_target_pairs={{4,0},{8,4},{12,8},{16,12},{20,16},{24,20},{28,24},{5,1},{9,5},{13... | collective-permute-start | bytes 589832 | tf_op jit(solution)/shard_map/ppermute | solution.py:17
  25.3 8.6 %collective-permute-start.2 = (bf16[96,64,16]{0,2,1:T(8,128)(2,1)}, bf16[96,64,16]{0,2,1:T(8,128)(2,1)}, u32[]{:S(2)}, u32[]{:S(2)}) collective-permute-start(bf16[96,64,16]{0,2,1:T(8,128)(2,1)} %copy.13), channel_id=1, source_target_pairs={{0,4},{4,8},{8,12},{12,16},{16,20},{20,24},{24,28},{1,5},{5,9},{9,... | collective-permute-start | bytes 589832 | tf_op jit(solution)/shard_map/ppermute | solution.py:14
  54.7 7.3 %collective-permute-start.4 = (bf16[16,64,128]{2,1,0:T(8,128)(2,1)S(1)}, bf16[16,64,128]{2,1,0:T(8,128)(2,1)S(1)}, u32[]{:S(2)}, u32[]{:S(2)}) collective-permute-start(bf16[16,64,128]{2,1,0:T(8,128)(2,1)S(1)} %get-tuple-element.39), channel_id=1, source_target_pairs={{0,32},{32,64},{64,96},{96,128},{128,160},{160,192},{192,224},{1,3... | collective-permute-start | bytes 786440 | tf_op jit(solution)/shard_map/ppermute | solution.py:14
  58.7 7.7 %collective-permute-start.5 = (bf16[16,64,128]{2,1,0:T(8,128)(2,1)S(1)}, bf16[16,64,128]{2,1,0:T(8,128)(2,1)S(1)}, u32[]{:S(2)}, u32[]{:S(2)}) collective-permute-start(bf16[16,64,128]{2,1,0:T(8,128)(2,1)S(1)} %get-tuple-element.40), channel_id=1, source_target_pairs={{32,0},{64,32},{96,64},{128,96},{160,128},{192,160},{224,192},{33,... | collective-permute-start | bytes 786440 | tf_op jit(solution)/shard_map/ppermute | solution.py:17
  71.6 11.7 %collective-permute-start.6 = (bf16[96,64,16]{0,2,1:T(8,128)(2,1)S(1)}, bf16[96,64,16]{0,2,1:T(8,128)(2,1)S(1)}, u32[]{:S(2)}, u32[]{:S(2)}) collective-permute-start(bf16[96,64,16]{0,2,1:T(8,128)(2,1)S(1)} %copy.18), channel_id=1, source_target_pairs={{0,4},{4,8},{8,12},{12,16},{16,20},{20,24},{24,28},{1,5},{5,9},{9,... | collective-permute-start | bytes 589832 | tf_op jit(solution)/shard_map/ppermute | solution.py:14
  79.4 7.6 %collective-permute-start.7 = (bf16[96,64,16]{0,2,1:T(8,128)(2,1)}, bf16[96,64,16]{0,2,1:T(8,128)(2,1)}, u32[]{:S(2)}, u32[]{:S(2)}) collective-permute-start(bf16[96,64,16]{0,2,1:T(8,128)(2,1)} %copy.19), channel_id=1, source_target_pairs={{4,0},{8,4},{12,8},{16,12},{20,16},{24,20},{28,24},{5,1},{9,5},{13... | collective-permute-start | bytes 589832 | tf_op jit(solution)/shard_map/ppermute | solution.py:17
  107.9 9.3 %collective-permute-start.9 = (bf16[16,64,128]{2,1,0:T(8,128)(2,1)S(1)}, bf16[16,64,128]{2,1,0:T(8,128)(2,1)S(1)}, u32[]{:S(2)}, u32[]{:S(2)}) collective-permute-start(bf16[16,64,128]{2,1,0:T(8,128)(2,1)S(1)} %get-tuple-element.37), channel_id=1, source_target_pairs={{0,32},{32,64},{64,96},{96,128},{128,160},{160,192},{192,224},{1,3... | collective-permute-start | bytes 786440 | tf_op jit(solution)/shard_map/ppermute | solution.py:14
  113.9 7.7 %collective-permute-start.10 = (bf16[16,64,128]{2,1,0:T(8,128)(2,1)S(1)}, bf16[16,64,128]{2,1,0:T(8,128)(2,1)S(1)}, u32[]{:S(2)}, u32[]{:S(2)}) collective-permute-start(bf16[16,64,128]{2,1,0:T(8,128)(2,1)S(1)} %get-tuple-element.38), channel_id=1, source_target_pairs={{32,0},{64,32},{96,64},{128,96},{160,128},{192,160},{224,192},{33,... | collective-permute-start | bytes 786440 | tf_op jit(solution)/shard_map/ppermute | solution.py:17
  126.8 9.3 %collective-permute-start.11 = (bf16[96,64,16]{0,2,1:T(8,128)(2,1)S(1)}, bf16[96,64,16]{0,2,1:T(8,128)(2,1)}, u32[]{:S(2)}, u32[]{:S(2)}) collective-permute-start(bf16[96,64,16]{0,2,1:T(8,128)(2,1)S(1)} %copy.24), channel_id=1, source_target_pairs={{0,4},{4,8},{8,12},{12,16},{16,20},{20,24},{24,28},{1,5},{5,9},{9,... | collective-permute-start | bytes 589832 | tf_op jit(solution)/shard_map/ppermute | solution.py:14
  134.7 8.7 %collective-permute-start.12 = (bf16[96,64,16]{0,2,1:T(8,128)(2,1)}, bf16[96,64,16]{0,2,1:T(8,128)(2,1)}, u32[]{:S(2)}, u32[]{:S(2)}) collective-permute-start(bf16[96,64,16]{0,2,1:T(8,128)(2,1)} %copy.25), channel_id=1, source_target_pairs={{4,0},{8,4},{12,8},{16,12},{20,16},{24,20},{28,24},{5,1},{9,5},{13... | collective-permute-start | bytes 589832 | tf_op jit(solution)/shard_map/ppermute | solution.py:17
  161.0 7.2 %collective-permute-start.13 = (bf16[16,64,128]{2,1,0:T(8,128)(2,1)S(1)}, bf16[16,64,128]{2,1,0:T(8,128)(2,1)S(1)}, u32[]{:S(2)}, u32[]{:S(2)}) collective-permute-start(bf16[16,64,128]{2,1,0:T(8,128)(2,1)S(1)} %get-tuple-element.35), channel_id=1, source_target_pairs={{0,32},{32,64},{64,96},{96,128},{128,160},{160,192},{192,224},{1,3... | collective-permute-start | bytes 786440 | tf_op jit(solution)/shard_map/ppermute | solution.py:14
  164.8 7.7 %collective-permute-start.14 = (bf16[16,64,128]{2,1,0:T(8,128)(2,1)S(1)}, bf16[16,64,128]{2,1,0:T(8,128)(2,1)S(1)}, u32[]{:S(2)}, u32[]{:S(2)}) collective-permute-start(bf16[16,64,128]{2,1,0:T(8,128)(2,1)S(1)} %get-tuple-element.36), channel_id=1, source_target_pairs={{32,0},{64,32},{96,64},{128,96},{160,128},{192,160},{224,192},{33,... | collective-permute-start | bytes 786440 | tf_op jit(solution)/shard_map/ppermute | solution.py:17
  177.7 11.3 %collective-permute-start.15 = (bf16[96,64,16]{0,2,1:T(8,128)(2,1)S(1)}, bf16[96,64,16]{0,2,1:T(8,128)(2,1)}, u32[]{:S(2)}, u32[]{:S(2)}) collective-permute-start(bf16[96,64,16]{0,2,1:T(8,128)(2,1)S(1)} %copy.28), channel_id=1, source_target_pairs={{0,4},{4,8},{8,12},{12,16},{16,20},{20,24},{24,28},{1,5},{5,9},{9,... | collective-permute-start | bytes 589832 | tf_op jit(solution)/shard_map/ppermute | solution.py:14
  187.7 7.4 %collective-permute-start.16 = (bf16[96,64,16]{0,2,1:T(8,128)(2,1)}, bf16[96,64,16]{0,2,1:T(8,128)(2,1)}, u32[]{:S(2)}, u32[]{:S(2)}) collective-permute-start(bf16[96,64,16]{0,2,1:T(8,128)(2,1)} %copy.29), channel_id=1, source_target_pairs={{4,0},{8,4},{12,8},{16,12},{20,16},{24,20},{28,24},{5,1},{9,5},{13... | collective-permute-start | bytes 589832 | tf_op jit(solution)/shard_map/ppermute | solution.py:17
  216.0 10.4 %collective-permute-start.18 = (bf16[16,64,128]{2,1,0:T(8,128)(2,1)S(1)}, bf16[16,64,128]{2,1,0:T(8,128)(2,1)S(1)}, u32[]{:S(2)}, u32[]{:S(2)}) collective-permute-start(bf16[16,64,128]{2,1,0:T(8,128)(2,1)S(1)} %get-tuple-element.33), channel_id=1, source_target_pairs={{0,32},{32,64},{64,96},{96,128},{128,160},{160,192},{192,224},{1,3... | collective-permute-start | bytes 786440 | tf_op jit(solution)/shard_map/ppermute | solution.py:14
  223.2 7.7 %collective-permute-start.19 = (bf16[16,64,128]{2,1,0:T(8,128)(2,1)S(1)}, bf16[16,64,128]{2,1,0:T(8,128)(2,1)S(1)}, u32[]{:S(2)}, u32[]{:S(2)}) collective-permute-start(bf16[16,64,128]{2,1,0:T(8,128)(2,1)S(1)} %get-tuple-element.34), channel_id=1, source_target_pairs={{32,0},{64,32},{96,64},{128,96},{160,128},{192,160},{224,192},{33,... | collective-permute-start | bytes 786440 | tf_op jit(solution)/shard_map/ppermute | solution.py:17
  236.0 7.8 %collective-permute-start.20 = (bf16[96,64,16]{0,2,1:T(8,128)(2,1)S(1)}, bf16[96,64,16]{0,2,1:T(8,128)(2,1)S(1)}, u32[]{:S(2)}, u32[]{:S(2)}) collective-permute-start(bf16[96,64,16]{0,2,1:T(8,128)(2,1)S(1)} %copy.33), channel_id=1, source_target_pairs={{0,4},{4,8},{8,12},{12,16},{16,20},{20,24},{24,28},{1,5},{5,9},{9,... | collective-permute-start | bytes 589832 | tf_op jit(solution)/shard_map/ppermute | solution.py:14
  242.3 7.4 %collective-permute-start.21 = (bf16[96,64,16]{0,2,1:T(8,128)(2,1)}, bf16[96,64,16]{0,2,1:T(8,128)(2,1)}, u32[]{:S(2)}, u32[]{:S(2)}) collective-permute-start(bf16[96,64,16]{0,2,1:T(8,128)(2,1)} %copy.34), channel_id=1, source_target_pairs={{4,0},{8,4},{12,8},{16,12},{20,16},{24,20},{28,24},{5,1},{9,5},{13... | collective-permute-start | bytes 589832 | tf_op jit(solution)/shard_map/ppermute | solution.py:17
  267.4 6.9 %collective-permute-start.22 = (bf16[16,64,128]{2,1,0:T(8,128)(2,1)S(1)}, bf16[16,64,128]{2,1,0:T(8,128)(2,1)S(1)}, u32[]{:S(2)}, u32[]{:S(2)}) collective-permute-start(bf16[16,64,128]{2,1,0:T(8,128)(2,1)S(1)} %get-tuple-element.31), channel_id=1, source_target_pairs={{0,32},{32,64},{64,96},{96,128},{128,160},{160,192},{192,224},{1,3... | collective-permute-start | bytes 786440 | tf_op jit(solution)/shard_map/ppermute | solution.py:14
  271.0 7.7 %collective-permute-start.23 = (bf16[16,64,128]{2,1,0:T(8,128)(2,1)S(1)}, bf16[16,64,128]{2,1,0:T(8,128)(2,1)S(1)}, u32[]{:S(2)}, u32[]{:S(2)}) collective-permute-start(bf16[16,64,128]{2,1,0:T(8,128)(2,1)S(1)} %get-tuple-element.32), channel_id=1, source_target_pairs={{32,0},{64,32},{96,64},{128,96},{160,128},{192,160},{224,192},{33,... | collective-permute-start | bytes 786440 | tf_op jit(solution)/shard_map/ppermute | solution.py:17
  284.6 7.5 %collective-permute-start.24 = (bf16[96,64,16]{0,2,1:T(8,128)(2,1)}, bf16[96,64,16]{0,2,1:T(8,128)(2,1)}, u32[]{:S(2)}, u32[]{:S(2)}) collective-permute-start(bf16[96,64,16]{0,2,1:T(8,128)(2,1)} %copy.37), channel_id=1, source_target_pairs={{0,4},{4,8},{8,12},{12,16},{16,20},{20,24},{24,28},{1,5},{5,9},{9,... | collective-permute-start | bytes 589832 | tf_op jit(solution)/shard_map/ppermute | solution.py:14
  290.9 7.4 %collective-permute-start.25 = (bf16[96,64,16]{0,2,1:T(8,128)(2,1)}, bf16[96,64,16]{0,2,1:T(8,128)(2,1)}, u32[]{:S(2)}, u32[]{:S(2)}) collective-permute-start(bf16[96,64,16]{0,2,1:T(8,128)(2,1)} %copy.38), channel_id=1, source_target_pairs={{4,0},{8,4},{12,8},{16,12},{20,16},{24,20},{28,24},{5,1},{9,5},{13... | collective-permute-start | bytes 589832 | tf_op jit(solution)/shard_map/ppermute | solution.py:17
  318.9 7.6 %collective-permute-start.27 = (bf16[16,64,128]{2,1,0:T(8,128)(2,1)S(1)}, bf16[16,64,128]{2,1,0:T(8,128)(2,1)S(1)}, u32[]{:S(2)}, u32[]{:S(2)}) collective-permute-start(bf16[16,64,128]{2,1,0:T(8,128)(2,1)S(1)} %get-tuple-element.29), channel_id=1, source_target_pairs={{0,32},{32,64},{64,96},{96,128},{128,160},{160,192},{192,224},{1,3... | collective-permute-start | bytes 786440 | tf_op jit(solution)/shard_map/ppermute | solution.py:14
  323.2 7.7 %collective-permute-start.28 = (bf16[16,64,128]{2,1,0:T(8,128)(2,1)S(1)}, bf16[16,64,128]{2,1,0:T(8,128)(2,1)S(1)}, u32[]{:S(2)}, u32[]{:S(2)}) collective-permute-start(bf16[16,64,128]{2,1,0:T(8,128)(2,1)S(1)} %get-tuple-element.30), channel_id=1, source_target_pairs={{32,0},{64,32},{96,64},{128,96},{160,128},{192,160},{224,192},{33,... | collective-permute-start | bytes 786440 | tf_op jit(solution)/shard_map/ppermute | solution.py:17
  337.0 6.8 %collective-permute-start.29 = (bf16[96,64,16]{0,2,1:T(8,128)(2,1)}, bf16[96,64,16]{0,2,1:T(8,128)(2,1)}, u32[]{:S(2)}, u32[]{:S(2)}) collective-permute-start(bf16[96,64,16]{0,2,1:T(8,128)(2,1)} %copy.42), channel_id=1, source_target_pairs={{0,4},{4,8},{8,12},{12,16},{16,20},{20,24},{24,28},{1,5},{5,9},{9,... | collective-permute-start | bytes 589832 | tf_op jit(solution)/shard_map/ppermute | solution.py:14
  342.3 7.4 %collective-permute-start.30 = (bf16[96,64,16]{0,2,1:T(8,128)(2,1)}, bf16[96,64,16]{0,2,1:T(8,128)(2,1)}, u32[]{:S(2)}, u32[]{:S(2)}) collective-permute-start(bf16[96,64,16]{0,2,1:T(8,128)(2,1)} %copy.43), channel_id=1, source_target_pairs={{4,0},{8,4},{12,8},{16,12},{20,16},{24,20},{28,24},{5,1},{9,5},{13... | collective-permute-start | bytes 589832 | tf_op jit(solution)/shard_map/ppermute | solution.py:17
  365.9 6.5 %collective-permute-start.31 = (bf16[16,64,128]{2,1,0:T(8,128)(2,1)S(1)}, bf16[16,64,128]{2,1,0:T(8,128)(2,1)S(1)}, u32[]{:S(2)}, u32[]{:S(2)}) collective-permute-start(bf16[16,64,128]{2,1,0:T(8,128)(2,1)S(1)} %get-tuple-element.27), channel_id=1, source_target_pairs={{0,32},{32,64},{64,96},{96,128},{128,160},{160,192},{192,224},{1,3... | collective-permute-start | bytes 786440 | tf_op jit(solution)/shard_map/ppermute | solution.py:14
  369.1 7.7 %collective-permute-start.32 = (bf16[16,64,128]{2,1,0:T(8,128)(2,1)S(1)}, bf16[16,64,128]{2,1,0:T(8,128)(2,1)S(1)}, u32[]{:S(2)}, u32[]{:S(2)}) collective-permute-start(bf16[16,64,128]{2,1,0:T(8,128)(2,1)S(1)} %get-tuple-element.28), channel_id=1, source_target_pairs={{32,0},{64,32},{96,64},{128,96},{160,128},{192,160},{224,192},{33,... | collective-permute-start | bytes 786440 | tf_op jit(solution)/shard_map/ppermute | solution.py:17
  383.3 7.9 %collective-permute-start.33 = (bf16[96,64,16]{0,2,1:T(8,128)(2,1)}, bf16[96,64,16]{0,2,1:T(8,128)(2,1)}, u32[]{:S(2)}, u32[]{:S(2)}) collective-permute-start(bf16[96,64,16]{0,2,1:T(8,128)(2,1)} %copy.46), channel_id=1, source_target_pairs={{0,4},{4,8},{8,12},{12,16},{16,20},{20,24},{24,28},{1,5},{5,9},{9,... | collective-permute-start | bytes 589832 | tf_op jit(solution)/shard_map/ppermute | solution.py:14
  389.9 7.4 %collective-permute-start.34 = (bf16[96,64,16]{0,2,1:T(8,128)(2,1)}, bf16[96,64,16]{0,2,1:T(8,128)(2,1)}, u32[]{:S(2)}, u32[]{:S(2)}) collective-permute-start(bf16[96,64,16]{0,2,1:T(8,128)(2,1)} %copy.47), channel_id=1, source_target_pairs={{4,0},{8,4},{12,8},{16,12},{20,16},{24,20},{28,24},{5,1},{9,5},{13... | collective-permute-start | bytes 589832 | tf_op jit(solution)/shard_map/ppermute | solution.py:17
  (18 other events, 262.4 us)
where the time goes:
time: 419 us; the launch traced here: 414 us
  local copies, waits for them, and re-layouts  173 us (41%)
  starting transfers between devices  101 us (24%)
  waiting for transfers between devices  72.1 us (17%)
  other arithmetic  40.6 us (10%)
  matrix products  21.1 us (5%)
  between operations  6.65 us (2%)
    ppermute x16, starting transfers between devices, extended(): lax.ppermute(lax.slice_in_dim(block, block.shape[dim] - width, None, axis...  70.9 us
    ppermute x16, waiting for transfers between devices, extended(): lax.ppermute(lax.slice_in_dim(block, 0, width, axis=dim), axis, backward)  50.4 us
    unnamed x90, local copies, waits for them, and re-layouts  42.4 us
    slice x24, local copies, waits for them, and re-layouts, extended(): lax.slice_in_dim(block, block.shape[dim] - width, None, axis=dim)  41.3 us
    concatenate x16, other arithmetic, extended(): block = jnp.concatenate([low, block, high], axis=dim)  34.1 us
    ppermute x8, local copies, waits for them, and re-layouts, extended(): lax.ppermute(lax.slice_in_dim(block, 0, width, axis=dim), axis, backward)  31.3 us
    ppermute x8, local copies, waits for them, and re-layouts, extended(): lax.ppermute(lax.slice_in_dim(block, block.shape[dim] - width, None, axis...  27.3 us
    ppermute x16, starting transfers between devices, extended(): lax.ppermute(lax.slice_in_dim(block, 0, width, axis=dim), axis, backward)  26.1 us
  transfers between devices with their start and end apart: 35, of which 26 were waited for; matrix products, arithmetic and copies ran while one was open for 12% of the time, Pallas kernels for 0%

commit v1 on v0

v1 whole, which is shorter than its diff:
```python
import functools

import jax
import jax.numpy as jnp
from jax import lax
from jax.experimental import pallas as pl
from jax.experimental.pallas import tpu as pltpu
from jax.sharding import PartitionSpec as P

MESH = pl.DeviceIdType.MESH
BF = jnp.bfloat16
F32 = jnp.float32
DMAX = 16
AROUND = [(dr, dc) for dr in (-1, 0, 1) for dc in (-1, 0, 1) if (dr, dc) != (0, 0)]
NINE = [(0, 0)] + AROUND
NT = (((1,), (1,)), ((), ()))


def kernel(
    shape,
    dil,
    pre,
    cot,
    occ,
    w,
    coup,
    out,
    pre_e,
    pre0,
    pack,
    rim,
    s_own,
    s_in,
    shifted,
    m0_e,
    pack0,
    rim0,
    shifted0,
    grad1,
    totals,
    pmap,
    cmap,
    q_tile,
    q_side,
    in_tile,
    in_side,
    in_row,
    in_corner,
    w1l,
    w0l,
    vb,
    cb,
    out_v,
    local_sem,
    a_send,
    a_recv,
    s_send,
    s_recv,
    q_send,
    q_recv,
    m_send,
    m_recv,
):
    n_row, n_col, n_level = shape
    rows, chans, cols = 64, 64, 128
    ext = rows + 2 * DMAX
    row = lax.axis_index("row")
    col = lax.axis_index("col")
    level = lax.axis_index("level")

    def exists(dr, dc):
        return (
            (row + dr >= 0) & (row + dr < n_row) & (col + dc >= 0) & (col + dc < n_col)
        )

    def peer(dr, dc, dl=0):
        return {"row": row + dr, "col": col + dc, "level": level + dl}

    def remote(src, dst, send, recv, device):
        return pltpu.make_async_remote_copy(
            src_ref=src,
            dst_ref=dst,
            send_sem=send,
            recv_sem=recv,
            device_id=device,
            device_id_type=MESH,
        )

    load1 = pltpu.make_async_copy(pre.at[1], pre_e.at[pl.ds(DMAX, rows)], local_sem.at[0])
    load0 = pltpu.make_async_copy(pre.at[0], pre0, local_sem.at[1])
    load1.start()
    load0.start()

    for ref in (s_in, in_tile, in_side, in_row, in_corner):
        ref[...] = jnp.zeros_like(ref)

    barrier = pltpu.get_barrier_semaphore()
    for dr, dc in AROUND:

        @pl.when(exists(dr, dc))
        def _():
            pl.semaphore_signal(barrier, inc=1, device_id=peer(dr, dc), device_id_type=MESH)

    for dr, dc in NINE:

        @pl.when(exists(dr, dc) & (level + 1 < n_level))
        def _():
            pl.semaphore_signal(
                barrier, inc=1, device_id=peer(dr, dc, 1), device_id_type=MESH
            )

    count_r = jnp.where(row > 0, 1, 0) + 1 + jnp.where(row + 1 < n_row, 1, 0)
    count_c = jnp.where(col > 0, 1, 0) + 1 + jnp.where(col + 1 < n_col, 1, 0)
    around = count_r * count_c
    expected = around - 1 + jnp.where(level > 0, around, 0)

    for side, cond in ((0, row == 0), (1, row + 1 == n_row)):

        @pl.when(cond)
        def _():
            span = pl.ds(0 if side == 0 else DMAX + rows, DMAX)
            pre_e[span] = jnp.zeros((DMAX, chans, cols), BF)
            m0_e[span] = jnp.zeros((DMAX, chans, cols), BF)
            groups = pl.ds(0 if side == 0 else 10, 2)
            for lr in (0, 1):
                rim[lr, groups] = jnp.zeros((2, chans, cols), BF)
                rim0[lr, groups] = jnp.zeros((2, chans, cols), BF)

    for side, cond in ((0, col == 0), (1, col + 1 == n_col)):

        @pl.when(cond)
        def _():
            rim[side] = jnp.zeros((12, chans, cols), BF)
            rim0[side] = jnp.zeros((12, chans, cols), BF)

    own = jnp.where(occ[...] > 0, cot[...].astype(F32), 0.0).astype(BF)
    s_own[...] = own
    s_in[1, pl.ds(DMAX, rows)] = own

    pl.semaphore_wait(barrier, expected)

    src_rows = {1: (48, 16), 0: (0, 64), -1: (0, 16)}
    dst_rows = {1: (0, 16), 0: (16, 64), -1: (80, 16)}
    src_grps = {1: (6, 2), 0: (0, 8), -1: (0, 2)}
    dst_grps = {1: (0, 2), 0: (2, 8), -1: (10, 2)}

    def small_copies():
        found = []
        for k, (dr, dc) in enumerate(AROUND):
            found.append(
                (
                    (dr, dc),
                    remote(
                        s_own.at[pl.ds(*src_rows[dr])],
                        s_in.at[1 - dc, pl.ds(*dst_rows[dr])],
                        s_send.at[k],
                        s_recv.at[k],
                        peer(dr, dc),
                    ),
                )
            )
        return found

    def rim_copies(source, full, packed, rims, send, recv, offset):
        found = []
        for k, (dr, dc) in enumerate(AROUND):
            if dc == 0:
                start, size = src_rows[dr]
                src = source.at[pl.ds(start + offset, size)]
                dst = full.at[pl.ds(*dst_rows[dr])]
            else:
                src = packed.at[1 if dc == 1 else 0, pl.ds(*src_grps[dr])]
                dst = rims.at[0 if dc == 1 else 1, pl.ds(*dst_grps[dr])]
            found.append(((dr, dc), remote(src, dst, send.at[k], recv.at[k], peer(dr, dc))))
        return found

    def start(copies, which):
        for (dr, dc), copy in copies:
            if which(dr, dc):

                @pl.when(exists(dr, dc))
                def _():
                    copy.start()

    def wait_recv(copies, which=lambda dr, dc: True):
        for (dr, dc), copy in copies:
            if which(dr, dc):

                @pl.when(exists(-dr, -dc))
                def _():
                    copy.wait_recv()

    def wait_send(copies):
        for (dr, dc), copy in copies:

            @pl.when(exists(dr, dc))
            def _():
                copy.wait_send()

    a_copies = rim_copies(pre.at[1], pre_e, pack, rim, a_send, a_recv, 0)
    s_copies = small_copies()
    start(a_copies, lambda dr, dc: dc == 0)
    start(s_copies, lambda dr, dc: True)

    lane = lax.broadcasted_iota(jnp.int32, (chans, cols), 1)
    lane_e = lax.broadcasted_iota(jnp.int32, (ext, cols), 1)

    def pack_group(source, base, target, g):
        left = jnp.zeros((chans, cols), BF)
        right = jnp.zeros((chans, cols), BF)
        for i in range(8):
            value = source[base + g * 8 + i]
            if i:
                value = pltpu.roll(value, 16 * i, 1)
            left = jnp.where(lane // 16 == i, value, left)
            right = jnp.where(lane // 16 == (i + 7) % 8, value, right)
        target[0, g] = left
        target[1, g] = right

    def unpacked(rims, g, i):
        value = jnp.where(lane // 16 == i, rims[1, g], rims[0, g])
        if i:
            value = pltpu.roll(value, cols - 16 * i, 1)
        return value

    def side_shift(tile, halo, index, d):
        if index == 0:
            return pltpu.roll(jnp.where(index_lane(tile) >= d, tile, halo), cols - d, 1)
        return pltpu.roll(jnp.where(index_lane(tile) < cols - d, tile, halo), d, 1)

    def index_lane(value):
        return lane if value.shape[0] == chans else lane_e

    d1 = dil[1]
    d0 = dil[0]

    load1.wait()

    @pl.loop(0, 8)
    def _(g):
        pack_group(pre_e, DMAX, pack, g)

    start(a_copies, lambda dr, dc: dc != 0)

    eye = jnp.where(
        lax.broadcasted_iota(jnp.int32, (chans, chans), 0)
        == lax.broadcasted_iota(jnp.int32, (chans, chans), 1),
        1.0,
        0.0,
    ).astype(F32)
    eye_b = eye.astype(BF)
    w1l[...] = lax.dot_general(eye_b, w[1], NT, preferred_element_type=F32).astype(BF)
    w0l[...] = lax.dot_general(eye_b, w[0], NT, preferred_element_type=F32).astype(BF)
    c0row = coup[0:1, :].astype(F32)
    c1row = coup[1:2, :].astype(F32)
    c0col = jnp.dot(
        (eye * c0row).astype(BF), jnp.ones((chans, cols), BF), preferred_element_type=F32
    )
    c0col_b = c0col.astype(BF)
    c1rows = jnp.broadcast_to(c1row, (8, chans)).astype(BF)
    diag = (
        lax.broadcasted_iota(jnp.int32, (8, 8 * chans), 1) // chans
        == lax.broadcasted_iota(jnp.int32, (8, 8 * chans), 0)
    )
    for t in range(9):
        wt = w[0, pl.ds(t * chans, chans), :]
        wide = lax.dot_general(
            c1rows, jnp.concatenate([wt] * 8, axis=0), NT, preferred_element_type=F32
        )
        vb[pl.ds(8 * t, 8), :] = jnp.where(diag, wide, 0.0)
    wide = lax.dot_general(
        c1rows, jnp.concatenate([eye_b] * 8, axis=0), NT, preferred_element_type=F32
    )
    cb[...] = jnp.where(diag, wide, 0.0)
    for t in range(9):
        pmap[t] = jnp.zeros((rows + 4 * DMAX, cols), F32)
    cmap[...] = jnp.zeros_like(cmap)

    wait_recv(a_copies)

    @pl.loop(0, 12)
    def _(g):
        for i in range(8):
            tile = pre_e[g * 8 + i]
            halo = unpacked(rim, g, i)
            tile = jnp.where(tile > 0, c0col_b, 0)
            halo = jnp.where(halo > 0, c0col_b, 0)
            e = g * 8 + i
            shifted[e, pl.ds(0, chans), :] = side_shift(tile, halo, 0, d1)
            shifted[e, pl.ds(chans, chans), :] = tile
            shifted[e, pl.ds(2 * chans, chans), :] = side_shift(tile, halo, 2, d1)

    load0.wait()
    wait_recv(s_copies)

    q_copies = []
    for k, (dr, dc) in enumerate(NINE):
        e_src = {1: (64, 32), 0: (0, 96), -1: (0, 32)}[dr]
        if dc == 0:
            src = q_tile.at[:, pl.ds(*e_src)]
            dst = in_tile if dr == 0 else in_row.at[(1 - dr) // 2]
        else:
            src = q_side.at[(1 - dc) // 2, pl.ds(*e_src)]
            dst = in_side.at[(1 - dc) // 2] if dr == 0 else in_corner.at[(1 - dc) // 2, (1 - dr) // 2]
        q_copies.append(((dr, dc), remote(src, dst, q_send.at[k], q_recv.at[k], peer(dr, dc, -1))))

    for (dr, dc), copy in q_copies:

        @pl.when(exists(-dr, -dc) & (level + 1 < n_level))
        def _():
            copy.wait_recv()

    low = lane_e < DMAX
    high = lane_e >= cols - DMAX
    gap = jnp.zeros((rows - 2 * DMAX, cols), F32)

    def around_rows(above, below):
        return jnp.concatenate([above.astype(F32), gap, below.astype(F32)], axis=0)

    left = in_side[0].astype(F32) + around_rows(in_corner[0, 0], in_corner[0, 1])
    right = in_side[1].astype(F32) + around_rows(in_corner[1, 0], in_corner[1, 1])
    tile = in_tile[0].astype(F32) + around_rows(in_row[0, 0], in_row[1, 0])
    tile += jnp.where(low, left, 0.0) + jnp.where(high, right, 0.0)
    tile += s_in[1].astype(F32)
    halo = in_tile[1].astype(F32) + around_rows(in_row[0, 1], in_row[1, 1])
    halo += jnp.where(low, right, 0.0) + jnp.where(high, left, 0.0)
    halo += jnp.where(low, s_in[2].astype(F32), s_in[0].astype(F32))
    totals[0] = side_shift(tile, halo, 0, d1)
    totals[1] = tile
    totals[2] = side_shift(tile, halo, 2, d1)

    @pl.loop(0, rows // 4)
    def _(step):
        wide_in = []
        for i in range(4):
            r = step * 4 + i
            parts = []
            for a in (-1, 0, 1):
                e = r + DMAX - a * d1
                for b in range(3):
                    line = jnp.broadcast_to(totals[b, pl.ds(e, 1), :], (chans, cols)).astype(BF)
                    parts.append(shifted[e, pl.ds(b * chans, chans), :] * line)
            wide_in.append(jnp.concatenate(parts, axis=0))
        result = jnp.dot(
            w1l[...], jnp.concatenate(wide_in, axis=1), preferred_element_type=F32
        )
        for i in range(4):
            r = step * 4 + i
            value = result[:, i * cols : (i + 1) * cols]
            value += c0col * totals[1, pl.ds(r + DMAX, 1), :]
            grad1[r] = value
            m0_e[r + DMAX] = jnp.where(pre0[r] > 0, value.astype(BF), 0)

    m_copies = rim_copies(m0_e, m0_e, pack0, rim0, m_send, m_recv, DMAX)
    @pl.when(level > 0)
    def _():
        @pl.loop(0, 8)
        def _(g):
            first = jnp.concatenate([m0_e[DMAX + g * 8 + i] for i in range(8)], axis=0)
            maps = jnp.dot(vb[...].astype(BF), first, preferred_element_type=F32)
            second = jnp.concatenate([grad1[g * 8 + i].astype(BF) for i in range(8)], axis=0)
            center = jnp.dot(cb[...].astype(BF), second, preferred_element_type=F32)
            at = pl.ds(pl.multiple_of(g * 8, 8) + 2 * DMAX, 8)
            for t in range(9):
                pmap[t, at, :] = maps[8 * t : 8 * t + 8]
            cmap[pl.ds(pl.multiple_of(g * 8, 8) + DMAX, 8), :] = center

        def column(b):
            found = None
            for a in (-1, 0, 1):
                piece = pmap[(a + 1) * 3 + b + 1, pl.ds(DMAX - a * d0, ext), :]
                found = piece if found is None else found + piece
            return found

        goes_left = pltpu.roll(column(-1), cols - d0, 1)
        goes_right = pltpu.roll(column(1), d0, 1)
        q0 = cmap[...] + column(0)
        q0 += jnp.where(lane_e < cols - d0, goes_left, 0.0)
        q0 += jnp.where(lane_e >= d0, goes_right, 0.0)
        q1 = jnp.where(lane_e >= cols - d0, goes_left, 0.0)
        q1 += jnp.where(lane_e < d0, goes_right, 0.0)
        q_tile[0] = q0.astype(BF)
        q_tile[1] = q1.astype(BF)
        q_side[0] = jnp.where(low, q1, jnp.where(high, q0, 0.0)).astype(BF)
        q_side[1] = jnp.where(high, q1, jnp.where(low, q0, 0.0)).astype(BF)
        for (dr, dc), copy in q_copies:

            @pl.when(exists(dr, dc))
            def _():
                copy.start()

    start(m_copies, lambda dr, dc: dc == 0)

    @pl.loop(0, 8)
    def _(g):
        pack_group(m0_e, DMAX, pack0, g)

    start(m_copies, lambda dr, dc: dc != 0)
    wait_recv(m_copies)

    @pl.loop(0, 12)
    def _(g):
        for i in range(8):
            e = g * 8 + i
            tile = m0_e[e]
            halo = unpacked(rim0, g, i)
            shifted0[e, pl.ds(0, chans), :] = side_shift(tile, halo, 0, d0)
            shifted0[e, pl.ds(chans, chans), :] = tile
            shifted0[e, pl.ds(2 * chans, chans), :] = side_shift(tile, halo, 2, d0)

    @pl.loop(0, rows // 4)
    def _(step):
        wide_in = []
        for i in range(4):
            r = step * 4 + i
            parts = [shifted0[r + DMAX - a * d0] for a in (-1, 0, 1)]
            wide_in.append(jnp.concatenate(parts, axis=0))
        result = jnp.dot(
            w0l[...], jnp.concatenate(wide_in, axis=1), preferred_element_type=F32
        )
        for i in range(4):
            r = step * 4 + i
            out_v[r] = (grad1[r] + result[:, i * cols : (i + 1) * cols]).astype(BF)

    store = pltpu.make_async_copy(out_v, out, local_sem.at[2])
    store.start()
    wait_send(a_copies)
    wait_send(s_copies)
    wait_send(m_copies)

    @pl.when(level > 0)
    def _():
        wait_send(q_copies)

    store.wait()


def solution(mesh):
    shape = (mesh.shape["row"], mesh.shape["col"], mesh.shape["level"])

    def on_device(pre_acts, pred_cot, occupancy, conv_weights, coupling, dilation):
        vmem = pl.BlockSpec(memory_space=pltpu.VMEM)
        hbm = pl.BlockSpec(memory_space=pl.ANY)
        smem = pl.BlockSpec(memory_space=pltpu.SMEM)
        dma = pltpu.SemaphoreType.DMA
        result = pl.pallas_call(
            functools.partial(kernel, shape),
            out_shape=jax.ShapeDtypeStruct((64, 64, 128), BF),
            in_specs=[smem, hbm, vmem, vmem, vmem, vmem],
            out_specs=hbm,
            scratch_shapes=[
                pltpu.VMEM((96, 64, 128), BF),
                pltpu.VMEM((64, 64, 128), BF),
                pltpu.VMEM((2, 8, 64, 128), BF),
                pltpu.VMEM((2, 12, 64, 128), BF),
                pltpu.VMEM((64, 128), BF),
                pltpu.VMEM((3, 96, 128), BF),
                pltpu.VMEM((96, 192, 128), BF),
                pltpu.VMEM((96, 64, 128), BF),
                pltpu.VMEM((2, 8, 64, 128), BF),
                pltpu.VMEM((2, 12, 64, 128), BF),
                pltpu.VMEM((96, 192, 128), BF),
                pltpu.VMEM((64, 64, 128), F32),
                pltpu.VMEM((3, 96, 128), F32),
                pltpu.VMEM((9, 128, 128), F32),
                pltpu.VMEM((96, 128), F32),
                pltpu.VMEM((2, 96, 128), BF),
                pltpu.VMEM((2, 96, 128), BF),
                pltpu.VMEM((2, 96, 128), BF),
                pltpu.VMEM((2, 96, 128), BF),
                pltpu.VMEM((2, 2, 32, 128), BF),
                pltpu.VMEM((2, 2, 32, 128), BF),
                pltpu.VMEM((64, 576), BF),
                pltpu.VMEM((64, 576), BF),
                pltpu.VMEM((72, 512), F32),
                pltpu.VMEM((8, 512), F32),
                pltpu.VMEM((64, 64, 128), BF),
                dma((3,)),
                dma((8,)),
                dma((8,)),
                dma((8,)),
                dma((8,)),
                dma((9,)),
                dma((9,)),
                dma((8,)),
                dma((8,)),
            ],
            compiler_params=pltpu.CompilerParams(
                collective_id=0, has_side_effects=True, vmem_limit_bytes=48 * 2**20
            ),
        )(
            dilation,
            pre_acts.reshape(2, 64, 64, 128),
            pred_cot.reshape(64, 128),
            occupancy.reshape(64, 128),
            conv_weights.reshape(2, 576, 64),
            coupling.reshape(2, 64),
        )
        return result[None]

    return jax.shard_map(
        on_device,
        mesh=mesh,
        in_specs=(
            P("level", None, "row", None, "col"),
            P("level", "row", "col"),
            P("level", "row", "col"),
            P("level", None, None, None, None, None),
            P("level", None, None),
            P(),
        ),
        out_specs=P("level", "row", None, "col"),
        check_vma=False,
    )
```

time: 419 us -> 75 us (0.18)
  the two profiles are of different devices: /device:TPU:1 before, /device:TPU:105 now
where the time goes in v1:
time: 75 us; the launch traced here: 74.7 us
  Pallas kernels  68.4 us (91%)
  local copies, waits for them, and re-layouts  6.31 us (8%)
    pallas_call x1, Pallas kernels, on_device(): pl.pallas_call(functools.partial(kernel, shape), out_shape=jax.ShapeDtype...  68.4 us
    unnamed x13, local copies, waits for them, and re-layouts  6.31 us

profile of v1, /device:TPU:105, one launch (start us, length us, event | category | flops | bytes accessed | tf_op | source)
XLA Modules:
  0.0 74.7 jit_solution(15058031801031292313)
XLA Ops:
  0.0 0.0 copy-start
  0.0 1.6 %copy-done = bf16[1,2,64,64,128]{4,3,2,1,0:T(8,128)(2,1)S(1)} copy-done((bf16[1,2,64,64,128]{4,3,2,1,0:T(8,128)(2,1)S(1)}, bf16[1,2,64,64,128]{4,3,2,1,0:T(8,128)(2,1)}, u32[]{:S(2)}) %copy-start) | copy-done | bytes 2097176
  1.6 0.0 copy-start.1
  1.6 1.0 %copy-done.1 = bf16[1,2,3,3,64,64]{5,4,3,2,1,0:T(8,128)(2,1)S(1)} copy-done((bf16[1,2,3,3,64,64]{5,4,3,2,1,0:T(8,128)(2,1)S(1)}, bf16[1,2,3,3,64,64]{5,4,3,2,1,0:T(8,128)(2,1)}, u32[]{:S(2)}) %copy-start.1) | copy-done | bytes 147480
  2.6 0.0 copy-start.2
  2.6 0.8 %copy-done.2 = s32[1,64,128]{2,1,0:T(8,128)S(1)} copy-done((s32[1,64,128]{2,1,0:T(8,128)S(1)}, s32[1,64,128]{2,1,0:T(8,128)}, u32[]{:S(2)}) %copy-start.2) | copy-done | bytes 32792
  3.3 0.0 copy-start.3
  3.3 0.7 copy-done.3
  4.0 0.0 copy-start.4
  4.0 0.7 copy-done.4
  4.7 0.0 copy-start.5
  4.7 0.7 copy-done.5
  5.3 68.4 %shard_map.64 = bf16[64,64,128]{2,1,0:T(8,128)(2,1)S(1)} custom-call(s32[2]{0:T(128)S(1)} %copy-done.4, bf16[2,64,64,128]{3,2,1,0:T(8,128)(2,1)S(1)} %bitcast.7, bf16[64,128]{1,0:T(8,128)(2,1)S(1)} %bitcast.10, s32[64,128]{1,0:T(8,128)S(1)} %bitcast.9, bf16[2,576,64]{2,1,0:T(8,128)(2,1)S(1)} %bitcast.8, bf16[2,64]{1,0:T(2,128)(2,1)S(1)} %bitcast.11), custom_call_target="tpu_custom_call" | custom-call | tf_op jit(solution)/shard_map/pallas_call | solution.py:446
  73.7 1.0 %copy.8 = bf16[1,64,64,128]{3,2,1,0:T(8,128)(2,1)} copy(bf16[1,64,64,128]{3,2,1,0:T(8,128)(2,1)S(1)} %bitcast.6) | data formatting | bytes 2097152
Async XLA Ops:
  0.0 1.6 %copy-start = (bf16[1,2,64,64,128]{4,3,2,1,0:T(8,128)(2,1)S(1)}, bf16[1,2,64,64,128]{4,3,2,1,0:T(8,128)(2,1)}, u32[]{:S(2)}) copy-start(bf16[1,2,64,64,128]{4,3,2,1,0:T(8,128)(2,1)} %param.6) | copy-start | bytes 6291460
  1.6 1.0 %copy-start.1 = (bf16[1,2,3,3,64,64]{5,4,3,2,1,0:T(8,128)(2,1)S(1)}, bf16[1,2,3,3,64,64]{5,4,3,2,1,0:T(8,128)(2,1)}, u32[]{:S(2)}) copy-start(bf16[1,2,3,3,64,64]{5,4,3,2,1,0:T(8,128)(2,1)} %param.9) | copy-start | bytes 442372
  2.6 0.8 %copy-start.2 = (s32[1,64,128]{2,1,0:T(8,128)S(1)}, s32[1,64,128]{2,1,0:T(8,128)}, u32[]{:S(2)}) copy-start(s32[1,64,128]{2,1,0:T(8,128)} %param.8) | copy-start | bytes 98308
  3.3 0.7 copy-start.3
  4.0 0.7 copy-start.4
  4.7 0.7 copy-start.5

commit v2 on v1

v2 whole, which is shorter than its diff:
```python
import functools

import jax
import jax.numpy as jnp
from jax import lax
from jax.experimental import pallas as pl
from jax.experimental.pallas import tpu as pltpu
from jax.sharding import PartitionSpec as P

MESH = pl.DeviceIdType.MESH
BF = jnp.bfloat16
F32 = jnp.float32
DMAX = 16
AROUND = [(dr, dc) for dr in (-1, 0, 1) for dc in (-1, 0, 1) if (dr, dc) != (0, 0)]
NINE = [(0, 0)] + AROUND
NT = (((1,), (1,)), ((), ()))


def kernel(
    shape,
    dil,
    pre,
    cot_hbm,
    occ_hbm,
    w_hbm,
    coup_hbm,
    out,
    cot,
    occ,
    w,
    coup,
    pre_e,
    pre0,
    pack,
    rim,
    s_own,
    s_in,
    shifted,
    m0,
    m0_e,
    pack0,
    rim0,
    grad1,
    totals,
    pmap,
    cmap,
    q_msg,
    q_side,
    in_tile,
    in_side,
    in_row,
    in_corner,
    w1l,
    w1t,
    tmap,
    tcen,
    w0o,
    vb,
    cb,
    out_v,
    local_sem,
    out_sem,
    a_send,
    a_recv,
    s_send,
    s_recv,
    q_send,
    q_recv,
    m_send,
    m_recv,
):
    n_row, n_col, n_level = shape
    rows, chans, cols = 64, 64, 128
    ext = rows + 2 * DMAX
    row = lax.axis_index("row")
    col = lax.axis_index("col")
    level = lax.axis_index("level")

    def exists(dr, dc):
        return (
            (row + dr >= 0) & (row + dr < n_row) & (col + dc >= 0) & (col + dc < n_col)
        )

    def peer(dr, dc, dl=0):
        return {"row": row + dr, "col": col + dc, "level": level + dl}

    def remote(src, dst, send, recv, device):
        return pltpu.make_async_remote_copy(
            src_ref=src,
            dst_ref=dst,
            send_sem=send,
            recv_sem=recv,
            device_id=device,
            device_id_type=MESH,
        )

    loads = [
        pltpu.make_async_copy(src, dst, local_sem.at[i])
        for i, (src, dst) in enumerate(
            (
                (pre.at[1], pre_e.at[pl.ds(DMAX, rows)]),
                (cot_hbm, cot),
                (occ_hbm, occ),
                (w_hbm, w),
                (coup_hbm, coup),
                (pre.at[0], pre0),
            )
        )
    ]
    for load in loads:
        load.start()

    for ref in (s_in, in_tile, in_side, in_row, in_corner):
        ref[...] = jnp.zeros_like(ref)

    barrier = pltpu.get_barrier_semaphore()
    for dr, dc in AROUND:

        @pl.when(exists(dr, dc))
        def _():
            pl.semaphore_signal(barrier, inc=1, device_id=peer(dr, dc), device_id_type=MESH)

    for dr, dc in NINE:

        @pl.when(exists(dr, dc) & (level + 1 < n_level))
        def _():
            pl.semaphore_signal(
                barrier, inc=1, device_id=peer(dr, dc, 1), device_id_type=MESH
            )

    count_r = jnp.where(row > 0, 1, 0) + 1 + jnp.where(row + 1 < n_row, 1, 0)
    count_c = jnp.where(col > 0, 1, 0) + 1 + jnp.where(col + 1 < n_col, 1, 0)
    around = count_r * count_c
    expected = around - 1 + jnp.where(level > 0, around, 0)

    for side, cond in ((0, row == 0), (1, row + 1 == n_row)):

        @pl.when(cond)
        def _():
            span = pl.ds(0 if side == 0 else DMAX + rows, DMAX)
            pre_e[span] = jnp.zeros((DMAX, chans, cols), BF)
            m0_e[span] = jnp.zeros((DMAX, chans, cols), BF)
            groups = pl.ds(0 if side == 0 else 10, 2)
            for lr in (0, 1):
                rim[lr, groups] = jnp.zeros((2, chans, cols), BF)

    for side, cond in ((0, col == 0), (1, col + 1 == n_col)):

        @pl.when(cond)
        def _():
            rim[side] = jnp.zeros((12, chans, cols), BF)
            rim0[1 - side] = jnp.zeros((8, chans, cols), BF)

    src_rows = {1: (48, 16), 0: (0, 64), -1: (0, 16)}
    dst_rows = {1: (0, 16), 0: (16, 64), -1: (80, 16)}

    def row_copy(source, full, send, recv, offset, dr):
        start, size = src_rows[dr]
        k = (1 - dr) // 2
        return remote(
            source.at[pl.ds(start + offset, size)],
            full.at[pl.ds(*dst_rows[dr])],
            send.at[k],
            recv.at[k],
            peer(dr, 0),
        )

    def corner_copy(packed, rims, send, recv, dr, dc):
        k = 2 + (1 - dr) + (1 - dc) // 2
        return remote(
            packed.at[(1 + dc) // 2, pl.ds(6 if dr == 1 else 0, 2)],
            rims.at[(1 - dc) // 2, pl.ds(0 if dr == 1 else 10, 2)],
            send.at[k],
            recv.at[k],
            peer(dr, dc),
        )

    def side_copy(packed, rims, send, recv, dc):
        return remote(
            packed.at[(1 + dc) // 2],
            rims.at[(1 - dc) // 2, pl.ds(2, 8)],
            send.at[6 + (1 - dc) // 2],
            recv.at[6 + (1 - dc) // 2],
            peer(0, dc),
        )

    def when_started(dr, dc, act):
        @pl.when(exists(dr, dc))
        def _():
            act()

    def when_expected(dr, dc, act):
        @pl.when(exists(-dr, -dc))
        def _():
            act()

    early_rows = {dr: row_copy(pre.at[1], pre_e, a_send, a_recv, 0, dr) for dr in (1, -1)}
    early_sides = {dc: side_copy(pack, rim, a_send, a_recv, dc) for dc in (1, -1)}
    early_corners = {
        (dr, dc): corner_copy(pack, rim, a_send, a_recv, dr, dc) for dr in (1, -1) for dc in (1, -1)
    }
    late_rows = {dr: row_copy(m0, m0_e, m_send, m_recv, 0, dr) for dr in (1, -1)}

    def late_side(chunk, dc):
        k = 2 + 4 * ((1 - dc) // 2) + chunk
        return remote(
            pack0.at[(1 + dc) // 2, pl.ds(2 * chunk, 2)],
            rim0.at[(1 + dc) // 2, pl.ds(2 * chunk, 2)],
            m_send.at[k],
            m_recv.at[k],
            peer(0, dc),
        )

    def start_late_rows():
        for dr, copy in late_rows.items():
            when_started(dr, 0, copy.start)

    lane = lax.broadcasted_iota(jnp.int32, (DMAX, cols), 1).astype(F32).astype(BF)
    lane = jnp.concatenate([lane] * (chans // DMAX), axis=0)
    lane_e = lax.broadcasted_iota(jnp.int32, (ext, cols), 1)
    lane_b = lax.broadcasted_iota(jnp.int32, (32, cols), 1)

    def pack_rows(values):
        turns = [values[0]]
        for i in range(1, 8):
            turns.append(pltpu.roll(values[i], 16 * i, 1))
        left, right = turns[7], turns[0]
        for i in range(6, -1, -1):
            inside = lane < 16 * (i + 1)
            left = jnp.where(inside, turns[i], left)
            right = jnp.where(inside, turns[i + 1], right)
        return left, right

    def unpacked(rims, g, i):
        value = jnp.where((lane >= 16 * i) & (lane < 16 * i + 16), rims[1, g], rims[0, g])
        if i:
            value = pltpu.roll(value, cols - 16 * i, 1)
        return value

    d1 = dil[1]
    d0 = dil[0]

    def splat(value):
        return jnp.full((chans, cols), value.astype(F32)).astype(BF)

    def side_shift(tile, halo, index, d):
        if tile.shape[0] == chans:
            where, split = lane, splat(d if index == 0 else cols - d)
        else:
            where, split = lane_e, d if index == 0 else cols - d
        if index == 0:
            return pltpu.roll(jnp.where(where >= split, tile, halo), cols - d, 1)
        return pltpu.roll(jnp.where(where < split, tile, halo), d, 1)

    loads[0].wait()

    @pl.loop(0, 4)
    def _(chunk):
        for half in (0, 1):
            g = 2 * chunk + half
            left, right = pack_rows([pre_e[DMAX + 8 * g + i] for i in range(8)])
            pack[0, g] = left
            pack[1, g] = right

    pl.semaphore_wait(barrier, expected)
    for dc, copy in early_sides.items():
        when_started(0, dc, copy.start)
    for dr, copy in early_rows.items():
        when_started(dr, 0, copy.start)
    for (dr, dc), copy in early_corners.items():
        when_started(dr, dc, copy.start)

    loads[1].wait()
    loads[2].wait()
    own = jnp.where(occ[...] > 0, cot[...].astype(F32), 0.0).astype(BF)
    s_own[...] = own
    s_in[1, pl.ds(DMAX, rows)] = own
    s_copies = []
    for k, (dr, dc) in enumerate(AROUND):
        copy = remote(
            s_own.at[pl.ds(*src_rows[dr])],
            s_in.at[1 - dc, pl.ds(*dst_rows[dr])],
            s_send.at[k],
            s_recv.at[k],
            peer(dr, dc),
        )
        s_copies.append(((dr, dc), copy))
        when_started(dr, dc, copy.start)

    loads[3].wait()
    loads[4].wait()
    eye = jnp.where(
        lax.broadcasted_iota(jnp.int32, (chans, chans), 0)
        == lax.broadcasted_iota(jnp.int32, (chans, chans), 1),
        1.0,
        0.0,
    ).astype(F32)
    eye_b = eye.astype(BF)

    def tap(t):
        return w[0, pl.ds(t * chans, chans), :]

    def turned(value):
        return lax.dot_general(eye_b, value, NT, preferred_element_type=F32).astype(BF)

    w1l[...] = turned(w[1])
    c0row = coup[0:1, :].astype(F32)
    c1row = coup[1:2, :].astype(F32)
    c0col = jnp.dot(
        (eye * c0row).astype(BF), jnp.ones((chans, cols), BF), preferred_element_type=F32
    )
    c0col_b = c0col.astype(BF)
    c1rows = jnp.broadcast_to(c1row, (8, chans))
    diag = (
        lax.broadcasted_iota(jnp.int32, (8, 8 * chans), 1) // chans
        == lax.broadcasted_iota(jnp.int32, (8, 8 * chans), 0)
    )
    heads = lax.dot_general(
        c1rows.astype(BF), w[0], NT, preferred_element_type=F32
    )
    for b in range(3):
        w0o[pl.ds(b * chans, chans), :] = turned(
            jnp.concatenate([tap(3 * a + b) for a in range(3)], axis=0)
        )

    def spread(value):
        return jnp.where(diag, jnp.concatenate([value] * 8, axis=1), 0.0)

    vb[...] = jnp.concatenate(
        [spread(heads[:, t * chans : (t + 1) * chans]) for t in range(9)], axis=0
    ).astype(BF)
    cb[...] = jnp.concatenate([spread(c1rows)] * 2, axis=0).astype(BF)
    for t in range(9):
        for start in (DMAX, 2 * DMAX + rows):
            pmap[t, pl.ds(start, DMAX), :] = jnp.zeros((DMAX, cols), F32)
            pmap[t, pl.ds(start - DMAX if start == DMAX else start + DMAX, DMAX), :] = (
                jnp.zeros((DMAX, cols), F32)
            )
    for start in (0, DMAX + rows):
        cmap[pl.ds(start, DMAX), :] = jnp.zeros((DMAX, cols), F32)

    for dr, copy in early_rows.items():
        when_expected(dr, 0, copy.wait_recv)
    for dc, copy in early_sides.items():
        when_expected(0, dc, copy.wait_recv)
    for (dr, dc), copy in early_corners.items():
        when_expected(dr, dc, copy.wait_recv)

    @pl.loop(0, 3)
    def _(part):
        for quarter in range(4):
            g = part * 4 + quarter
            for i in range(8):
                e = g * 8 + i
                tile = jnp.where(pre_e[e] > 0, c0col_b, 0)
                halo = jnp.where(unpacked(rim, g, i) > 0, c0col_b, 0)
                shifted[e, pl.ds(0, chans), :] = side_shift(tile, halo, 0, d1)
                shifted[e, pl.ds(chans, chans), :] = tile
                shifted[e, pl.ds(2 * chans, chans), :] = side_shift(tile, halo, 2, d1)

    loads[5].wait()

    middle = (level > 0) & (level + 1 < n_level)

    @pl.when(middle)
    def _():
        for t in range(9):
            w1t[t] = turned(w[1, pl.ds(t * chans, chans), :])

        @pl.loop(0, 4)
        def _(chunk):
            keep = [pre0[chunk * 16 + i] > 0 for i in range(16)]
            for t in range(10):
                if t < 9:
                    taps_in = jnp.concatenate(
                        [
                            shifted[
                                chunk * 16 + i + DMAX - (t // 3 - 1) * d1,
                                pl.ds((t % 3) * chans, chans),
                                :,
                            ]
                            for i in range(16)
                        ],
                        axis=1,
                    )
                    made = jnp.dot(w1t[t], taps_in, preferred_element_type=F32).astype(BF)
                    pieces = [made[:, i * cols : (i + 1) * cols] for i in range(16)]
                else:
                    pieces = [c0col_b] * 16
                kept = [jnp.where(keep[i], pieces[i], 0) for i in range(16)]
                for target, lhs, values in ((tmap, vb, kept), (tcen, cb, pieces)):
                    rhs = jnp.concatenate(
                        [
                            jnp.concatenate(values[0:8], axis=0),
                            jnp.concatenate(values[8:16], axis=0),
                        ],
                        axis=1,
                    )
                    maps = jnp.dot(lhs[...], rhs, preferred_element_type=F32)
                    size = target.shape[2]
                    target[t, 2 * chunk] = maps[0:size, 0:cols]
                    target[t, 2 * chunk + 1] = maps[0:size, cols : 2 * cols]

    for (dr, dc), copy in s_copies:
        when_expected(dr, dc, copy.wait_recv)

    q_copies = []
    for k, (dr, dc) in enumerate(NINE):
        if dc == 0:
            src = q_msg.at[pl.ds(*{1: (96, 64), 0: (32, 128), -1: (0, 64)}[dr])]
            dst = in_tile if dr == 0 else in_row.at[(1 - dr) // 2]
        else:
            src = q_side.at[(1 - dc) // 2]
            dst = in_side.at[(1 - dc) // 2] if dr == 0 else in_corner.at[(1 - dc) // 2, (1 - dr) // 2]
        q_copies.append(((dr, dc), remote(src, dst, q_send.at[k], q_recv.at[k], peer(dr, dc, -1))))

    for (dr, dc), copy in q_copies:

        @pl.when(exists(-dr, -dc) & (level + 1 < n_level))
        def _():
            copy.wait_recv()

    low = lane_e < DMAX
    high = lane_e >= cols - DMAX

    def folded(value):
        found = None
        for j in range(3):
            piece = pltpu.roll(value[32 * j : 32 * j + 32], DMAX + 32 * j, 1)
            found = piece if found is None else jnp.where(lane_b // 32 == j, piece, found)
        return found

    def unfolded(value, j):
        return pltpu.roll(value.astype(F32), cols - DMAX - 32 * j, 1)

    def summed(middle, above, below):
        return jnp.concatenate(
            [
                unfolded(middle, 0) + unfolded(above, 2),
                unfolded(middle, 1),
                unfolded(middle, 2) + unfolded(below, 0),
            ],
            axis=0,
        )

    left = summed(in_side[0], in_corner[0, 0], in_corner[0, 1])
    right = summed(in_side[1], in_corner[1, 0], in_corner[1, 1])
    edges = jnp.concatenate(
        [
            in_row[0, pl.ds(0, 32)].astype(F32),
            jnp.zeros((rows - 2 * DMAX, cols), F32),
            in_row[1, pl.ds(32, 32)].astype(F32),
        ],
        axis=0,
    )
    tile = in_tile[pl.ds(0, ext)].astype(F32) + edges + s_in[1].astype(F32)
    tile += jnp.where(low, left, 0.0) + jnp.where(high, right, 0.0)
    halo = summed(in_tile[pl.ds(ext, 32)], in_row[0, pl.ds(32, 32)], in_row[1, pl.ds(0, 32)])
    halo += jnp.where(low, right + s_in[2].astype(F32), left + s_in[0].astype(F32))
    totals[0] = side_shift(tile, halo, 0, d1)
    totals[1] = tile
    totals[2] = side_shift(tile, halo, 2, d1)

    def layer_1(chunk):
        for pair in range(8):
            wide_in = []
            for i in range(2):
                r = chunk * 16 + pair * 2 + i
                parts = []
                for a in (-1, 0, 1):
                    e = r + DMAX - a * d1
                    for b in range(3):
                        line = jnp.broadcast_to(totals[b, pl.ds(e, 1), :], (16, cols)).astype(BF)
                        line = jnp.concatenate([line] * 4, axis=0)
                        parts.append(shifted[e, pl.ds(b * chans, chans), :] * line)
                wide_in.append(jnp.concatenate(parts, axis=0))
            result = jnp.dot(
                w1l[...], jnp.concatenate(wide_in, axis=1), preferred_element_type=F32
            )
            for i in range(2):
                r = chunk * 16 + pair * 2 + i
                value = result[:, i * cols : (i + 1) * cols]
                value += c0col * totals[1, pl.ds(r + DMAX, 1), :]
                grad1[r] = value
                kept = jnp.where(pre0[r] > 0, value.astype(BF), 0)
                m0[r] = kept
                m0_e[r + DMAX] = kept

    def prediction_maps(chunk):
        for half in range(2):
            g = chunk * 2 + half
            first = jnp.concatenate([m0[g * 8 + i] for i in range(8)], axis=0)
            maps = jnp.dot(vb[...], first, preferred_element_type=F32)
            second = jnp.concatenate([grad1[g * 8 + i].astype(BF) for i in range(8)], axis=0)
            center = jnp.dot(cb[...], second, preferred_element_type=F32)
            at = pl.ds(pl.multiple_of(g * 8, 8) + 2 * DMAX, 8)
            for t in range(9):
                pmap[t, at, :] = maps[8 * t : 8 * t + 8]
            cmap[pl.ds(pl.multiple_of(g * 8, 8) + DMAX, 8), :] = center[0:8]

    def column(b):
        found = None
        for a in (-1, 0, 1):
            piece = pmap[(a + 1) * 3 + b + 1, pl.ds(DMAX - a * d0, ext), :]
            found = piece if found is None else found + piece
        return found

    @pl.when(level + 1 == n_level)
    def _():
        @pl.loop(0, 4)
        def _(chunk):
            layer_1(chunk)
            prediction_maps(chunk)

    @pl.when(middle)
    def _():
        @pl.loop(0, 4)
        def _(chunk):
            for half in range(2):
                g = chunk * 2 + half
                lines = [
                    totals[t % 3, pl.ds(g * 8 + DMAX - (t // 3 - 1) * d1, 8), :]
                    for t in range(9)
                ]
                lines.append(totals[1, pl.ds(pl.multiple_of(g * 8, 8) + DMAX, 8), :])
                start = pl.multiple_of(g * 8, 8)
                for k in range(9):
                    found = lines[0] * tmap[0, g, pl.ds(8 * k, 8), :]
                    for t in range(1, 10):
                        found += lines[t] * tmap[t, g, pl.ds(8 * k, 8), :]
                    pmap[k, pl.ds(start + 2 * DMAX, 8), :] = found
                found = lines[0] * tcen[0, g]
                for t in range(1, 10):
                    found += lines[t] * tcen[t, g]
                cmap[pl.ds(start + DMAX, 8), :] = found

    @pl.when(level > 0)
    def _():
        goes_left = pltpu.roll(column(-1), cols - d0, 1)
        goes_right = pltpu.roll(column(1), d0, 1)
        q0 = cmap[...] + column(0)
        q0 += jnp.where(lane_e < cols - d0, goes_left, 0.0)
        q0 += jnp.where(lane_e >= d0, goes_right, 0.0)
        q1 = jnp.where(lane_e >= cols - d0, goes_left, 0.0)
        q1 += jnp.where(lane_e < d0, goes_right, 0.0)
        q_side[0] = folded(jnp.where(low, q1, q0)).astype(BF)
        q_side[1] = folded(jnp.where(low, q0, q1)).astype(BF)
        rim_part = folded(q1).astype(BF)
        q_msg[pl.ds(0, 32)] = rim_part
        q_msg[pl.ds(32, ext)] = q0.astype(BF)
        q_msg[pl.ds(32 + ext, 32)] = rim_part
        for (dr, dc), copy in q_copies:
            when_started(dr, dc, copy.start)

    @pl.when(level + 1 < n_level)
    def _():
        @pl.loop(0, 4)
        def _(step):
            layer_1(jnp.where(step == 0, 0, jnp.where(step == 1, 3, step - 1)))

            @pl.when(step == 1)
            def _():
                start_late_rows()

    @pl.when(level + 1 == n_level)
    def _():
        start_late_rows()

    edge = (lane < DMAX) | (lane >= cols - DMAX)
    own_right = lane >= splat(d0)
    own_left = lane < splat(cols - d0)

    def store(chunk):
        span = pl.ds(chunk * 16, 16)
        return pltpu.make_async_copy(out_v.at[span], out.at[span], out_sem.at[chunk])

    def layer_0(chunk, source, offset):
        outer = []
        for pair in range(8):
            wide_in = []
            for i in range(2):
                r = chunk * 16 + pair * 2 + i
                wide_in.append(
                    jnp.concatenate([source[r + offset - a * d0] for a in (-1, 0, 1)], axis=0)
                )
            result = jnp.dot(
                w0o[...], jnp.concatenate(wide_in, axis=1), preferred_element_type=F32
            )
            for i in range(2):
                r = chunk * 16 + pair * 2 + i
                lanes = slice(i * cols, (i + 1) * cols)
                goes_left = pltpu.roll(result[0:chans, lanes].astype(BF), cols - d0, 1)
                goes_right = pltpu.roll(result[2 * chans :, lanes].astype(BF), d0, 1)
                outer.append(jnp.where(own_right, jnp.where(own_left, 0, goes_left), goes_right))
                value = grad1[r] + result[chans : 2 * chans, lanes]
                value += jnp.where(own_left, goes_left, 0).astype(F32)
                value += jnp.where(own_right, goes_right, 0).astype(F32)
                grad1[r] = value
        for half in range(2):
            to_right, to_left = pack_rows(outer[8 * half : 8 * half + 8])
            pack0[0, 2 * chunk + half] = to_left
            pack0[1, 2 * chunk + half] = to_right
        for dc in (1, -1):
            when_started(0, dc, late_side(chunk, dc).start)

    @pl.loop(0, 2)
    def _(step):
        layer_0(step + 1, m0, 0)

    for dr, copy in late_rows.items():
        when_expected(dr, 0, copy.wait_recv)

    @pl.loop(0, 2)
    def _(step):
        layer_0(step * 3, m0_e, DMAX)

    @pl.loop(0, 4)
    def _(step):
        chunk = jnp.where(step < 2, step + 1, jnp.where(step == 2, 0, 3))
        for dc in (1, -1):
            when_expected(0, dc, late_side(chunk, dc).wait_recv)
        for half in range(2):
            g = chunk * 2 + half
            for i in range(8):
                r = g * 8 + i
                extra = jnp.where(edge, unpacked(rim0, g, i), 0).astype(F32)
                out_v[r] = (grad1[r] + extra).astype(BF)
        store(chunk).start()

    for dr, copy in early_rows.items():
        when_started(dr, 0, copy.wait_send)
    for dc, copy in early_sides.items():
        when_started(0, dc, copy.wait_send)
    for (dr, dc), copy in early_corners.items():
        when_started(dr, dc, copy.wait_send)
    for dr, copy in late_rows.items():
        when_started(dr, 0, copy.wait_send)
    for dc in (1, -1):
        for chunk in range(4):
            when_started(0, dc, late_side(chunk, dc).wait_send)
    for (dr, dc), copy in s_copies:
        when_started(dr, dc, copy.wait_send)

    @pl.when(level > 0)
    def _():
        for (dr, dc), copy in q_copies:
            when_started(dr, dc, copy.wait_send)

    for chunk in range(4):
        store(chunk).wait()


def solution(mesh):
    shape = (mesh.shape["row"], mesh.shape["col"], mesh.shape["level"])

    def on_device(pre_acts, pred_cot, occupancy, conv_weights, coupling, dilation):
        hbm = pl.BlockSpec(memory_space=pl.ANY)
        smem = pl.BlockSpec(memory_space=pltpu.SMEM)
        dma = pltpu.SemaphoreType.DMA
        result = pl.pallas_call(
            functools.partial(kernel, shape),
            out_shape=jax.ShapeDtypeStruct((64, 64, 128), BF),
            in_specs=[smem, hbm, hbm, hbm, hbm, hbm],
            out_specs=hbm,
            scratch_shapes=[
                pltpu.VMEM((64, 128), BF),
                pltpu.VMEM((64, 128), jnp.int32),
                pltpu.VMEM((2, 576, 64), BF),
                pltpu.VMEM((2, 64), BF),
                pltpu.VMEM((96, 64, 128), BF),
                pltpu.VMEM((64, 64, 128), BF),
                pltpu.VMEM((2, 8, 64, 128), BF),
                pltpu.VMEM((2, 12, 64, 128), BF),
                pltpu.VMEM((64, 128), BF),
                pltpu.VMEM((3, 96, 128), BF),
                pltpu.VMEM((96, 192, 128), BF),
                pltpu.VMEM((64, 64, 128), BF),
                pltpu.VMEM((96, 64, 128), BF),
                pltpu.VMEM((2, 8, 64, 128), BF),
                pltpu.VMEM((2, 8, 64, 128), BF),
                pltpu.VMEM((64, 64, 128), F32),
                pltpu.VMEM((3, 96, 128), F32),
                pltpu.VMEM((9, 128, 128), F32),
                pltpu.VMEM((96, 128), F32),
                pltpu.VMEM((160, 128), BF),
                pltpu.VMEM((2, 32, 128), BF),
                pltpu.VMEM((128, 128), BF),
                pltpu.VMEM((2, 32, 128), BF),
                pltpu.VMEM((2, 64, 128), BF),
                pltpu.VMEM((2, 2, 32, 128), BF),
                pltpu.VMEM((64, 576), BF),
                pltpu.VMEM((9, 64, 64), BF),
                pltpu.VMEM((10, 8, 72, 128), F32),
                pltpu.VMEM((10, 8, 8, 128), F32),
                pltpu.VMEM((192, 192), BF),
                pltpu.VMEM((72, 512), BF),
                pltpu.VMEM((16, 512), BF),
                pltpu.VMEM((64, 64, 128), BF),
                dma((6,)),
                dma((4,)),
                dma((8,)),
                dma((8,)),
                dma((8,)),
                dma((8,)),
                dma((9,)),
                dma((9,)),
                dma((10,)),
                dma((10,)),
            ],
            compiler_params=pltpu.CompilerParams(
                collective_id=0, has_side_effects=True, vmem_limit_bytes=64 * 2**20
            ),
        )(
            dilation,
            pre_acts.reshape(2, 64, 64, 128),
            pred_cot.reshape(64, 128),
            occupancy.reshape(64, 128),
            conv_weights.reshape(2, 576, 64),
            coupling.reshape(2, 64),
        )
        return result[None]

    return jax.shard_map(
        on_device,
        mesh=mesh,
        in_specs=(
            P("level", None, "row", None, "col"),
            P("level", "row", "col"),
            P("level", "row", "col"),
            P("level", None, None, None, None, None),
            P("level", None, None),
            P(),
        ),
        out_specs=P("level", "row", None, "col"),
        check_vma=False,
    )
```

time: 75 us -> 54.4 us (0.73)
  the two profiles are of different devices: /device:TPU:105 before, /device:TPU:1 now
where the time goes in v2:
time: 54.4 us; the launch traced here: 54.2 us
  Pallas kernels  52 us (96%)
  local copies, waits for them, and re-layouts  2.26 us (4%)
    pallas_call x1, Pallas kernels, on_device(): pl.pallas_call(functools.partial(kernel, shape), out_shape=jax.ShapeDtype...  52 us
    unnamed x1, local copies, waits for them, and re-layouts  2.26 us

profile of v2, /device:TPU:1, one launch (start us, length us, event | category | flops | bytes accessed | tf_op | source)
XLA Modules:
  0.0 54.2 jit_solution(15755442996289620850)
XLA Ops:
  0.0 52.0 %shard_map.64 = bf16[64,64,128]{2,1,0:T(8,128)(2,1)} custom-call(s32[2]{0:T(128)} %dil.1, bf16[2,64,64,128]{3,2,1,0:T(8,128)(2,1)} %bitcast.7, bf16[64,128]{1,0:T(8,128)(2,1)} %bitcast.10, s32[64,128]{1,0:T(8,128)} %bitcast.9, bf16[2,576,64]{2,1,0:T(8,128)(2,1)} %bitcast.8, bf16[2,64]{1,0:T(2,128)(2,1)} %bitcast.11), custom_call_target="tpu_custom_call" | custom-call | tf_op jit(solution)/shard_map/pallas_call | solution.py:660
  52.0 2.3 %copy.8 = bf16[1,64,64,128]{3,2,1,0:T(8,128)(2,1)} copy(bf16[1,64,64,128]{3,2,1,0:T(8,128)(2,1)} %bitcast.6) | data formatting | bytes 2097152

commit v3 on v2

--- a/solution.py
+++ b/solution.py
@@ -154,19 +154,23 @@
     src_rows = {1: (48, 16), 0: (0, 64), -1: (0, 16)}
     dst_rows = {1: (0, 16), 0: (16, 64), -1: (80, 16)}
 
-    def row_copy(source, full, send, recv, offset, dr):
-        start, size = src_rows[dr]
-        k = (1 - dr) // 2
-        return remote(
-            source.at[pl.ds(start + offset, size)],
-            full.at[pl.ds(*dst_rows[dr])],
-            send.at[k],
-            recv.at[k],
-            peer(dr, 0),
-        )
+    def row_copies(source, full, send, recv):
+        found = []
+        for dr in (1, -1):
+            for part in range(4):
+                k = 4 * ((1 - dr) // 2) + part
+                copy = remote(
+                    source.at[pl.ds(src_rows[dr][0] + 4 * part, 4)],
+                    full.at[pl.ds(dst_rows[dr][0] + 4 * part, 4)],
+                    send.at[k],
+                    recv.at[k],
+                    peer(dr, 0),
+                )
+                found.append((dr, copy))
+        return found
 
     def corner_copy(packed, rims, send, recv, dr, dc):
-        k = 2 + (1 - dr) + (1 - dc) // 2
+        k = 8 + (1 - dr) + (1 - dc) // 2
         return remote(
             packed.at[(1 + dc) // 2, pl.ds(6 if dr == 1 else 0, 2)],
             rims.at[(1 - dc) // 2, pl.ds(0 if dr == 1 else 10, 2)],
@@ -175,12 +179,13 @@
             peer(dr, dc),
         )
 
-    def side_copy(packed, rims, send, recv, dc):
+    def side_copy(packed, rims, send, recv, dc, chunk):
+        k = 12 + 4 * ((1 - dc) // 2) + chunk
         return remote(
-            packed.at[(1 + dc) // 2],
-            rims.at[(1 - dc) // 2, pl.ds(2, 8)],
-            send.at[6 + (1 - dc) // 2],
-            recv.at[6 + (1 - dc) // 2],
+            packed.at[(1 + dc) // 2, pl.ds(2 * chunk, 2)],
+            rims.at[(1 - dc) // 2, pl.ds(2 * chunk + 2, 2)],
+            send.at[k],
+            recv.at[k],
             peer(0, dc),
         )
 
@@ -194,15 +199,17 @@
         def _():
             act()
 
-    early_rows = {dr: row_copy(pre.at[1], pre_e, a_send, a_recv, 0, dr) for dr in (1, -1)}
-    early_sides = {dc: side_copy(pack, rim, a_send, a_recv, dc) for dc in (1, -1)}
-    early_corners = {
-        (dr, dc): corner_copy(pack, rim, a_send, a_recv, dr, dc) for dr in (1, -1) for dc in (1, -1)
-    }
-    late_rows = {dr: row_copy(m0, m0_e, m_send, m_recv, 0, dr) for dr in (1, -1)}
+    early = [((dr, 0), copy) for dr, copy in row_copies(pre.at[1], pre_e, a_send, a_recv)]
+    for chunk in range(4):
+        for dc in (1, -1):
+            early.append(((0, dc), side_copy(pack, rim, a_send, a_recv, dc, chunk)))
+    for dr in (1, -1):
+        for dc in (1, -1):
+            early.append(((dr, dc), corner_copy(pack, rim, a_send, a_recv, dr, dc)))
+    late_rows = row_copies(m0, m0_e, m_send, m_recv)
 
     def late_side(chunk, dc):
-        k = 2 + 4 * ((1 - dc) // 2) + chunk
+        k = 8 + 4 * ((1 - dc) // 2) + chunk
         return remote(
             pack0.at[(1 + dc) // 2, pl.ds(2 * chunk, 2)],
             rim0.at[(1 + dc) // 2, pl.ds(2 * chunk, 2)],
@@ -211,14 +218,15 @@
             peer(0, dc),
         )
 
-    def start_late_rows():
-        for dr, copy in late_rows.items():
-            when_started(dr, 0, copy.start)
+    def start_late_rows(which):
+        for dr, copy in late_rows:
+            if dr == which:
+                when_started(dr, 0, copy.start)
 
     lane = lax.broadcasted_iota(jnp.int32, (DMAX, cols), 1).astype(F32).astype(BF)
     lane = jnp.concatenate([lane] * (chans // DMAX), axis=0)
     lane_e = lax.broadcasted_iota(jnp.int32, (ext, cols), 1)
-    lane_b = lax.broadcasted_iota(jnp.int32, (32, cols), 1)
+    lane_b = lax.broadcasted_iota(jnp.int32, (8, cols), 1)
 
     def pack_rows(values):
         turns = [values[0]]
@@ -263,11 +271,7 @@
             pack[1, g] = right
 
     pl.semaphore_wait(barrier, expected)
-    for dc, copy in early_sides.items():
-        when_started(0, dc, copy.start)
-    for dr, copy in early_rows.items():
-        when_started(dr, 0, copy.start)
-    for (dr, dc), copy in early_corners.items():
+    for (dr, dc), copy in early:
         when_started(dr, dc, copy.start)
 
     loads[1].wait()
@@ -339,11 +343,7 @@
     for start in (0, DMAX + rows):
         cmap[pl.ds(start, DMAX), :] = jnp.zeros((DMAX, cols), F32)
 
-    for dr, copy in early_rows.items():
-        when_expected(dr, 0, copy.wait_recv)
-    for dc, copy in early_sides.items():
-        when_expected(0, dc, copy.wait_recv)
-    for (dr, dc), copy in early_corners.items():
+    for (dr, dc), copy in early:
         when_expected(dr, dc, copy.wait_recv)
 
     @pl.loop(0, 3)
@@ -407,11 +407,14 @@
     q_copies = []
     for k, (dr, dc) in enumerate(NINE):
         if dc == 0:
-            src = q_msg.at[pl.ds(*{1: (96, 64), 0: (32, 128), -1: (0, 64)}[dr])]
+            src = q_msg.at[pl.ds(*{1: (80, 48), 0: (16, 128), -1: (0, 48)}[dr])]
             dst = in_tile if dr == 0 else in_row.at[(1 - dr) // 2]
+        elif dr == 0:
+            src = q_side.at[(1 - dc) // 2]
+            dst = in_side.at[(1 - dc) // 2]
         else:
-            src = q_side.at[(1 - dc) // 2]
-            dst = in_side.at[(1 - dc) // 2] if dr == 0 else in_corner.at[(1 - dc) // 2, (1 - dr) // 2]
+            src = q_side.at[(1 - dc) // 2, pl.ds(0, 16)]
+            dst = in_corner.at[(1 - dc) // 2, (1 - dr) // 2]
         q_copies.append(((dr, dc), remote(src, dst, q_send.at[k], q_recv.at[k], peer(dr, dc, -1))))
 
     for (dr, dc), copy in q_copies:
@@ -424,21 +427,30 @@
     high = lane_e >= cols - DMAX
 
     def folded(value):
-        found = None
-        for j in range(3):
-            piece = pltpu.roll(value[32 * j : 32 * j + 32], DMAX + 32 * j, 1)
-            found = piece if found is None else jnp.where(lane_b // 32 == j, piece, found)
-        return found
-
-    def unfolded(value, j):
-        return pltpu.roll(value.astype(F32), cols - DMAX - 32 * j, 1)
+        found = []
+        for j in (0, 2, 1):
+            block = value[32 * j : 32 * j + 8]
+            block = pltpu.roll(block, DMAX, 1)
+            for m in range(1, 4):
+                start = 32 * j + 8 * m
+                piece = pltpu.roll(value[start : start + 8], (DMAX + 32 * m) % cols, 1)
+                block = jnp.where(lane_b // 32 == m, piece, block)
+            found.append(block)
+        found.append(jnp.zeros((8, cols), F32))
+        return jnp.concatenate(found, axis=0).astype(BF)
+
+    def unfolded(block):
+        return jnp.concatenate(
+            [pltpu.roll(block, (cols - DMAX - 32 * m) % cols, 1) for m in range(4)], axis=0
+        )
 
     def summed(middle, above, below):
+        middle, above, below = (part.astype(F32) for part in (middle, above, below))
         return jnp.concatenate(
             [
-                unfolded(middle, 0) + unfolded(above, 2),
-                unfolded(middle, 1),
-                unfolded(middle, 2) + unfolded(below, 0),
+                unfolded(middle[0:8]) + unfolded(above[8:16]),
+                unfolded(middle[16:24]),
+                unfolded(middle[8:16]) + unfolded(below[0:8]),
             ],
             axis=0,
         )
@@ -449,13 +461,13 @@
         [
             in_row[0, pl.ds(0, 32)].astype(F32),
             jnp.zeros((rows - 2 * DMAX, cols), F32),
-            in_row[1, pl.ds(32, 32)].astype(F32),
+            in_row[1, pl.ds(16, 32)].astype(F32),
         ],
         axis=0,
     )
     tile = in_tile[pl.ds(0, ext)].astype(F32) + edges + s_in[1].astype(F32)
     tile += jnp.where(low, left, 0.0) + jnp.where(high, right, 0.0)
-    halo = summed(in_tile[pl.ds(ext, 32)], in_row[0, pl.ds(32, 32)], in_row[1, pl.ds(0, 32)])
+    halo = summed(in_tile[pl.ds(ext, 32)], in_row[0, pl.ds(32, 16)], in_row[1, pl.ds(0, 16)])
     halo += jnp.where(low, right + s_in[2].astype(F32), left + s_in[0].astype(F32))
     totals[0] = side_shift(tile, halo, 0, d1)
     totals[1] = tile
@@ -543,12 +555,12 @@
         q0 += jnp.where(lane_e >= d0, goes_right, 0.0)
         q1 = jnp.where(lane_e >= cols - d0, goes_left, 0.0)
         q1 += jnp.where(lane_e < d0, goes_right, 0.0)
-        q_side[0] = folded(jnp.where(low, q1, q0)).astype(BF)
-        q_side[1] = folded(jnp.where(low, q0, q1)).astype(BF)
-        rim_part = folded(q1).astype(BF)
-        q_msg[pl.ds(0, 32)] = rim_part
-        q_msg[pl.ds(32, ext)] = q0.astype(BF)
-        q_msg[pl.ds(32 + ext, 32)] = rim_part
+        q_side[0] = folded(jnp.where(low, q1, q0))
+        q_side[1] = folded(jnp.where(low, q0, q1))
+        rim_part = folded(q1)
+        q_msg[pl.ds(0, DMAX)] = rim_part[0:DMAX]
+        q_msg[pl.ds(DMAX, ext)] = q0.astype(BF)
+        q_msg[pl.ds(DMAX + ext, 32)] = rim_part
         for (dr, dc), copy in q_copies:
             when_started(dr, dc, copy.start)
 
@@ -558,13 +570,18 @@
         def _(step):
             layer_1(jnp.where(step == 0, 0, jnp.where(step == 1, 3, step - 1)))
 
+            @pl.when(step == 0)
+            def _():
+                start_late_rows(-1)
+
             @pl.when(step == 1)
             def _():
-                start_late_rows()
+                start_late_rows(1)
 
     @pl.when(level + 1 == n_level)
     def _():
-        start_late_rows()
+        start_late_rows(-1)
+        start_late_rows(1)
 
     edge = (lane < DMAX) | (lane >= cols - DMAX)
     own_right = lane >= splat(d0)
@@ -607,7 +624,7 @@
     def _(step):
         layer_0(step + 1, m0, 0)
 
-    for dr, copy in late_rows.items():
+    for dr, copy in late_rows:
         when_expected(dr, 0, copy.wait_recv)
 
     @pl.loop(0, 2)
@@ -627,13 +644,9 @@
                 out_v[r] = (grad1[r] + extra).astype(BF)
         store(chunk).start()
 
-    for dr, copy in early_rows.items():
-        when_started(dr, 0, copy.wait_send)
-    for dc, copy in early_sides.items():
-        when_started(0, dc, copy.wait_send)
-    for (dr, dc), copy in early_corners.items():
+    for (dr, dc), copy in early:
         when_started(dr, dc, copy.wait_send)
-    for dr, copy in late_rows.items():
+    for dr, copy in late_rows:
         when_started(dr, 0, copy.wait_send)
     for dc in (1, -1):
         for chunk in range(4):
@@ -682,12 +695,12 @@
                 pltpu.VMEM((3, 96, 128), F32),
                 pltpu.VMEM((9, 128, 128), F32),
                 pltpu.VMEM((96, 128), F32),
-                pltpu.VMEM((160, 128), BF),
+                pltpu.VMEM((144, 128), BF),
                 pltpu.VMEM((2, 32, 128), BF),
                 pltpu.VMEM((128, 128), BF),
                 pltpu.VMEM((2, 32, 128), BF),
-                pltpu.VMEM((2, 64, 128), BF),
-                pltpu.VMEM((2, 2, 32, 128), BF),
+                pltpu.VMEM((2, 48, 128), BF),
+                pltpu.VMEM((2, 2, 16, 128), BF),
                 pltpu.VMEM((64, 576), BF),
                 pltpu.VMEM((9, 64, 64), BF),
                 pltpu.VMEM((10, 8, 72, 128), F32),
@@ -698,14 +711,14 @@
                 pltpu.VMEM((64, 64, 128), BF),
                 dma((6,)),
                 dma((4,)),
-                dma((8,)),
-                dma((8,)),
+                dma((20,)),
+                dma((20,)),
                 dma((8,)),
                 dma((8,)),
                 dma((9,)),
                 dma((9,)),
-                dma((10,)),
-                dma((10,)),
+                dma((16,)),
+                dma((16,)),
             ],
             compiler_params=pltpu.CompilerParams(
                 collective_id=0, has_side_effects=True, vmem_limit_bytes=64 * 2**20

time: 54.4 us -> 53.7 us (0.987)
  Pallas kernels: 52 us -> 51.3 us
    pallas_call x1, Pallas kernels: 52 us -> 51.3 us  [on_device(): pl.pallas_call(functools.partial(kernel, shape), out_shape=jax.ShapeDtype...]
where the time goes in v3:
time: 53.7 us; the launch traced here: 53.6 us
  Pallas kernels  51.3 us (96%)
  local copies, waits for them, and re-layouts  2.26 us (4%)
    pallas_call x1, Pallas kernels, on_device(): pl.pallas_call(functools.partial(kernel, shape), out_shape=jax.ShapeDtype...  51.3 us
    unnamed x1, local copies, waits for them, and re-layouts  2.26 us

profile of v3, /device:TPU:1, one launch (start us, length us, event | category | flops | bytes accessed | tf_op | source)
XLA Modules:
  0.0 53.6 jit_solution(7368255217159457804)
XLA Ops:
  0.0 51.3 %shard_map.64 = bf16[64,64,128]{2,1,0:T(8,128)(2,1)} custom-call(s32[2]{0:T(128)} %dil.1, bf16[2,64,64,128]{3,2,1,0:T(8,128)(2,1)} %bitcast.7, bf16[64,128]{1,0:T(8,128)(2,1)} %bitcast.10, s32[64,128]{1,0:T(8,128)} %bitcast.9, bf16[2,576,64]{2,1,0:T(8,128)(2,1)} %bitcast.8, bf16[2,64]{1,0:T(2,128)(2,1)} %bitcast.11), custom_call_target="tpu_custom_call" | custom-call | tf_op jit(solution)/shard_map/pallas_call | solution.py:673
  51.3 2.3 %copy.8 = bf16[1,64,64,128]{3,2,1,0:T(8,128)(2,1)} copy(bf16[1,64,64,128]{3,2,1,0:T(8,128)(2,1)} %bitcast.6) | data formatting | bytes 2097152

commit v4 on v3

--- a/solution.py
+++ b/solution.py
@@ -36,8 +36,11 @@
     s_own,
     s_in,
     shifted,
-    m0,
     m0_e,
+    m0_rows,
+    pack_c,
+    rim_c,
+    outside,
     pack0,
     rim0,
     grad1,
@@ -55,6 +58,11 @@
     tmap,
     tcen,
     w0o,
+    w0r,
+    pmat,
+    smat,
+    umat,
+    omat,
     vb,
     cb,
     out_v,
@@ -139,29 +147,31 @@
         def _():
             span = pl.ds(0 if side == 0 else DMAX + rows, DMAX)
             pre_e[span] = jnp.zeros((DMAX, chans, cols), BF)
-            m0_e[span] = jnp.zeros((DMAX, chans, cols), BF)
+            m0_rows[side] = jnp.zeros((DMAX, chans, cols), BF)
             groups = pl.ds(0 if side == 0 else 10, 2)
             for lr in (0, 1):
                 rim[lr, groups] = jnp.zeros((2, chans, cols), BF)
+                rim_c[lr, pl.ds(2 * side, 2)] = jnp.zeros((2, chans, cols), BF)
 
     for side, cond in ((0, col == 0), (1, col + 1 == n_col)):
 
         @pl.when(cond)
         def _():
             rim[side] = jnp.zeros((12, chans, cols), BF)
+            rim_c[side] = jnp.zeros((4, chans, cols), BF)
             rim0[1 - side] = jnp.zeros((8, chans, cols), BF)
 
     src_rows = {1: (48, 16), 0: (0, 64), -1: (0, 16)}
     dst_rows = {1: (0, 16), 0: (16, 64), -1: (80, 16)}
 
-    def row_copies(source, full, send, recv):
+    def row_copies(source, targets, send, recv):
         found = []
         for dr in (1, -1):
             for part in range(4):
                 k = 4 * ((1 - dr) // 2) + part
                 copy = remote(
                     source.at[pl.ds(src_rows[dr][0] + 4 * part, 4)],
-                    full.at[pl.ds(dst_rows[dr][0] + 4 * part, 4)],
+                    targets[dr].at[pl.ds(4 * part, 4)],
                     send.at[k],
                     recv.at[k],
                     peer(dr, 0),
@@ -199,14 +209,33 @@
         def _():
             act()
 
-    early = [((dr, 0), copy) for dr, copy in row_copies(pre.at[1], pre_e, a_send, a_recv)]
+    early = [((dr, 0), copy) for dr, copy in row_copies(
+        pre.at[1],
+        {dr: pre_e.at[pl.ds(*dst_rows[dr])] for dr in (1, -1)},
+        a_send,
+        a_recv,
+    )]
     for chunk in range(4):
         for dc in (1, -1):
             early.append(((0, dc), side_copy(pack, rim, a_send, a_recv, dc, chunk)))
     for dr in (1, -1):
         for dc in (1, -1):
             early.append(((dr, dc), corner_copy(pack, rim, a_send, a_recv, dr, dc)))
-    late_rows = row_copies(m0, m0_e, m_send, m_recv)
+    late_rows = row_copies(
+        m0_e.at[pl.ds(DMAX, rows)], {1: m0_rows.at[0], -1: m0_rows.at[1]}, m_send, m_recv
+    )
+    late_corners = []
+    for dr in (1, -1):
+        for dc in (1, -1):
+            k = 16 + (1 - dr) + (1 - dc) // 2
+            copy = remote(
+                pack_c.at[(1 + dc) // 2, pl.ds(2 if dr == 1 else 0, 2)],
+                rim_c.at[(1 - dc) // 2, pl.ds(0 if dr == 1 else 2, 2)],
+                m_send.at[k],
+                m_recv.at[k],
+                peer(dr, dc),
+            )
+            late_corners.append(((dr, dc), copy))
 
     def late_side(chunk, dc):
         k = 8 + 4 * ((1 - dc) // 2) + chunk
@@ -218,44 +247,60 @@
             peer(0, dc),
         )
 
-    def start_late_rows(which):
-        for dr, copy in late_rows:
-            if dr == which:
-                when_started(dr, 0, copy.start)
-
     lane = lax.broadcasted_iota(jnp.int32, (DMAX, cols), 1).astype(F32).astype(BF)
     lane = jnp.concatenate([lane] * (chans // DMAX), axis=0)
     lane_e = lax.broadcasted_iota(jnp.int32, (ext, cols), 1)
     lane_b = lax.broadcasted_iota(jnp.int32, (8, cols), 1)
 
+    def picks(size, *wanted):
+        k = lax.broadcasted_iota(jnp.int32, (size, wanted[0].shape[1]), 0)
+        found = k == wanted[0]
+        for other in wanted[1:]:
+            found = found | (k == other)
+        return jnp.where(found, 1.0, 0.0).astype(BF)
+
+    n_wide = lax.broadcasted_iota(jnp.int32, (1, 2 * cols), 1)
+    n_one = lax.broadcasted_iota(jnp.int32, (1, cols), 1)
+    w_wide = jnp.where(n_wide < cols, n_wide, n_wide - cols)
+    group = w_wide // 16
+    inner = w_wide % 16
+    pmat[...] = picks(
+        8 * cols,
+        jnp.where(
+            n_wide < cols,
+            group * cols + inner,
+            ((group + 1) % 8) * cols + cols - DMAX + inner,
+        ),
+    )
+
     def pack_rows(values):
-        turns = [values[0]]
-        for i in range(1, 8):
-            turns.append(pltpu.roll(values[i], 16 * i, 1))
-        left, right = turns[7], turns[0]
-        for i in range(6, -1, -1):
-            inside = lane < 16 * (i + 1)
-            left = jnp.where(inside, turns[i], left)
-            right = jnp.where(inside, turns[i + 1], right)
-        return left, right
-
-    def unpacked(rims, g, i):
-        value = jnp.where((lane >= 16 * i) & (lane < 16 * i + 16), rims[1, g], rims[0, g])
-        if i:
-            value = pltpu.roll(value, cols - 16 * i, 1)
-        return value
+        both = jnp.dot(
+            jnp.concatenate(values, axis=1), pmat[...], preferred_element_type=F32
+        ).astype(BF)
+        return both[:, 0:cols], both[:, cols:]
+
+    def send_outer(which):
+        for dr, copy in late_rows:
+            if dr == which:
+                when_started(dr, 0, copy.start)
+        for half in (0, 1):
+            g = half + (6 if which == 1 else 0)
+            left, right = pack_rows([m0_e[DMAX + 8 * g + i] for i in range(8)])
+            slot = half + (2 if which == 1 else 0)
+            pack_c[0, slot] = left
+            pack_c[1, slot] = right
+        for (dr, dc), copy in late_corners:
+            if dr == which:
+                when_started(dr, dc, copy.start)
+
+    def merged(rims, g, i):
+        return jnp.where((lane >= 16 * i) & (lane < 16 * i + 16), rims[1, g], rims[0, g])
 
     d1 = dil[1]
     d0 = dil[0]
 
-    def splat(value):
-        return jnp.full((chans, cols), value.astype(F32)).astype(BF)
-
     def side_shift(tile, halo, index, d):
-        if tile.shape[0] == chans:
-            where, split = lane, splat(d if index == 0 else cols - d)
-        else:
-            where, split = lane_e, d if index == 0 else cols - d
+        where, split = lane_e, d if index == 0 else cols - d
         if index == 0:
             return pltpu.roll(jnp.where(where >= split, tile, halo), cols - d, 1)
         return pltpu.roll(jnp.where(where < split, tile, halo), d, 1)
@@ -327,6 +372,46 @@
             jnp.concatenate([tap(3 * a + b) for a in range(3)], axis=0)
         )
 
+    for layer, d in ((1, d1), (0, d0)):
+        right = n_wide + d
+        left = w_wide - d
+        for i in range(8):
+            smat[layer, i] = picks(
+                2 * cols,
+                jnp.where(
+                    n_wide < cols,
+                    jnp.where(right < cols, right, right + 16 * i),
+                    jnp.where(left >= 0, left, cols + ((left + 16 * i + cols) % cols)),
+                ),
+            )
+    for i in range(8):
+        umat[i] = picks(
+            cols,
+            jnp.where(
+                n_one < DMAX,
+                n_one + 16 * i,
+                jnp.where(n_one >= cols - DMAX, (n_one + 16 * i) % cols, -1),
+            ),
+        )
+    omat[...] = picks(
+        2 * cols,
+        jnp.where(
+            n_wide < cols,
+            jnp.where(w_wide + d0 < cols, w_wide + d0, -1),
+            jnp.where(w_wide >= cols - d0, w_wide + d0 - cols, -1),
+        ),
+        jnp.where(
+            n_wide < cols,
+            jnp.where(w_wide >= d0, cols + w_wide - d0, -1),
+            jnp.where(w_wide < d0, 2 * cols + w_wide - d0, -1),
+        ),
+    )
+    w0r[0] = turned(w[0, pl.ds(6 * chans, 3 * chans), :])
+    w0r[1] = turned(w[0, pl.ds(0, 3 * chans), :])
+    for side in (0, 1):
+        m0_e[pl.ds(side * (DMAX + rows), DMAX)] = jnp.zeros((DMAX, chans, cols), BF)
+        outside[side, pl.ds(16 - 16 * side, 16)] = jnp.zeros((DMAX, 3 * chans, cols), BF)
+
     def spread(value):
         return jnp.where(diag, jnp.concatenate([value] * 8, axis=1), 0.0)
 
@@ -348,15 +433,23 @@
 
     @pl.loop(0, 3)
     def _(part):
-        for quarter in range(4):
-            g = part * 4 + quarter
-            for i in range(8):
+        for i in range(8):
+            wide_in = []
+            for quarter in range(4):
+                g = part * 4 + quarter
                 e = g * 8 + i
                 tile = jnp.where(pre_e[e] > 0, c0col_b, 0)
-                halo = jnp.where(unpacked(rim, g, i) > 0, c0col_b, 0)
-                shifted[e, pl.ds(0, chans), :] = side_shift(tile, halo, 0, d1)
+                halo = jnp.where(merged(rim, g, i) > 0, c0col_b, 0)
                 shifted[e, pl.ds(chans, chans), :] = tile
-                shifted[e, pl.ds(2 * chans, chans), :] = side_shift(tile, halo, 2, d1)
+                wide_in.append(jnp.concatenate([tile, halo], axis=1))
+            both = jnp.dot(
+                jnp.concatenate(wide_in, axis=0), smat[1, i], preferred_element_type=F32
+            ).astype(BF)
+            for quarter in range(4):
+                e = (part * 4 + quarter) * 8 + i
+                here = both[quarter * chans : (quarter + 1) * chans]
+                shifted[e, pl.ds(0, chans), :] = here[:, 0:cols]
+                shifted[e, pl.ds(2 * chans, chans), :] = here[:, cols:]
 
     loads[5].wait()
 
@@ -495,13 +588,12 @@
                 value += c0col * totals[1, pl.ds(r + DMAX, 1), :]
                 grad1[r] = value
                 kept = jnp.where(pre0[r] > 0, value.astype(BF), 0)
-                m0[r] = kept
                 m0_e[r + DMAX] = kept
 
     def prediction_maps(chunk):
         for half in range(2):
             g = chunk * 2 + half
-            first = jnp.concatenate([m0[g * 8 + i] for i in range(8)], axis=0)
+            first = jnp.concatenate([m0_e[DMAX + g * 8 + i] for i in range(8)], axis=0)
             maps = jnp.dot(vb[...], first, preferred_element_type=F32)
             second = jnp.concatenate([grad1[g * 8 + i].astype(BF) for i in range(8)], axis=0)
             center = jnp.dot(cb[...], second, preferred_element_type=F32)
@@ -572,47 +664,58 @@
 
             @pl.when(step == 0)
             def _():
-                start_late_rows(-1)
+                send_outer(-1)
 
             @pl.when(step == 1)
             def _():
-                start_late_rows(1)
+                send_outer(1)
 
     @pl.when(level + 1 == n_level)
     def _():
-        start_late_rows(-1)
-        start_late_rows(1)
-
-    edge = (lane < DMAX) | (lane >= cols - DMAX)
-    own_right = lane >= splat(d0)
-    own_left = lane < splat(cols - d0)
+        send_outer(-1)
+        send_outer(1)
 
     def store(chunk):
         span = pl.ds(chunk * 16, 16)
         return pltpu.make_async_copy(out_v.at[span], out.at[span], out_sem.at[chunk])
 
-    def layer_0(chunk, source, offset):
+    @pl.loop(0, 4)
+    def _(chunk):
         outer = []
         for pair in range(8):
             wide_in = []
             for i in range(2):
                 r = chunk * 16 + pair * 2 + i
                 wide_in.append(
-                    jnp.concatenate([source[r + offset - a * d0] for a in (-1, 0, 1)], axis=0)
+                    jnp.concatenate([m0_e[r + DMAX - a * d0] for a in (-1, 0, 1)], axis=0)
                 )
             result = jnp.dot(
                 w0o[...], jnp.concatenate(wide_in, axis=1), preferred_element_type=F32
             )
+            moved = jnp.dot(
+                jnp.concatenate(
+                    [
+                        jnp.concatenate(
+                            [
+                                result[0:chans, i * cols : (i + 1) * cols],
+                                result[2 * chans :, i * cols : (i + 1) * cols],
+                            ],
+                            axis=1,
+                        )
+                        for i in range(2)
+                    ],
+                    axis=0,
+                ).astype(BF),
+                omat[...],
+                preferred_element_type=F32,
+            )
             for i in range(2):
                 r = chunk * 16 + pair * 2 + i
-                lanes = slice(i * cols, (i + 1) * cols)
-                goes_left = pltpu.roll(result[0:chans, lanes].astype(BF), cols - d0, 1)
-                goes_right = pltpu.roll(result[2 * chans :, lanes].astype(BF), d0, 1)
-                outer.append(jnp.where(own_right, jnp.where(own_left, 0, goes_left), goes_right))
-                value = grad1[r] + result[chans : 2 * chans, lanes]
-                value += jnp.where(own_left, goes_left, 0).astype(F32)
-                value += jnp.where(own_right, goes_right, 0).astype(F32)
-                grad1[r] = value
+                here = moved[i * chans : (i + 1) * chans]
+                outer.append(here[:, cols:].astype(BF))
+                grad1[r] = (
+                    grad1[r] + result[chans : 2 * chans, i * cols : (i + 1) * cols] + here[:, 0:cols]
+                )
         for half in range(2):
             to_right, to_left = pack_rows(outer[8 * half : 8 * half + 8])
             pack0[0, 2 * chunk + half] = to_left
@@ -620,34 +723,68 @@
         for dc in (1, -1):
             when_started(0, dc, late_side(chunk, dc).start)
 
-    @pl.loop(0, 2)
-    def _(step):
-        layer_0(step + 1, m0, 0)
+    def finish(chunk, more):
+        for dc in (1, -1):
+            when_expected(0, dc, late_side(chunk, dc).wait_recv)
+        for i in range(8):
+            extra = jnp.dot(
+                jnp.concatenate([merged(rim0, chunk * 2 + half, i) for half in range(2)], axis=0),
+                umat[i],
+                preferred_element_type=F32,
+            )
+            for half in range(2):
+                r = chunk * 16 + half * 8 + i
+                value = grad1[r] + extra[half * chans : (half + 1) * chans]
+                if more is not None:
+                    value += more[8 * half + i]
+                out_v[r] = value.astype(BF)
+        store(chunk).start()
+
+    @pl.loop(1, 3)
+    def _(chunk):
+        finish(chunk, None)
 
     for dr, copy in late_rows:
         when_expected(dr, 0, copy.wait_recv)
+    for (dr, dc), copy in late_corners:
+        when_expected(dr, dc, copy.wait_recv)
 
     @pl.loop(0, 2)
-    def _(step):
-        layer_0(step * 3, m0_e, DMAX)
-
-    @pl.loop(0, 4)
-    def _(step):
-        chunk = jnp.where(step < 2, step + 1, jnp.where(step == 2, 0, 3))
-        for dc in (1, -1):
-            when_expected(0, dc, late_side(chunk, dc).wait_recv)
-        for half in range(2):
-            g = chunk * 2 + half
-            for i in range(8):
-                r = g * 8 + i
-                extra = jnp.where(edge, unpacked(rim0, g, i), 0).astype(F32)
-                out_v[r] = (grad1[r] + extra).astype(BF)
-        store(chunk).start()
+    def _(side):
+        for i in range(8):
+            wide_in = []
+            for half in range(2):
+                tile = m0_rows[side, 8 * half + i]
+                halo = merged(rim_c, 2 * side + half, i)
+                outside[side, 16 * side + 8 * half + i, pl.ds(chans, chans), :] = tile
+                wide_in.append(jnp.concatenate([tile, halo], axis=1))
+            both = jnp.dot(
+                jnp.concatenate(wide_in, axis=0), smat[0, i], preferred_element_type=F32
+            ).astype(BF)
+            for half in range(2):
+                e = 16 * side + 8 * half + i
+                here = both[half * chans : (half + 1) * chans]
+                outside[side, e, pl.ds(0, chans), :] = here[:, 0:cols]
+                outside[side, e, pl.ds(2 * chans, chans), :] = here[:, cols:]
+
+    @pl.loop(0, 2)
+    def _(side):
+        first = jnp.where(side == 0, DMAX - d0, d0)
+        more = []
+        for pair in range(8):
+            wide_in = [outside[side, first + pair * 2 + i] for i in range(2)]
+            result = jnp.dot(
+                w0r[side], jnp.concatenate(wide_in, axis=1), preferred_element_type=F32
+            )
+            more += [result[:, i * cols : (i + 1) * cols] for i in range(2)]
+        finish(3 * side, more)
 
     for (dr, dc), copy in early:
         when_started(dr, dc, copy.wait_send)
     for dr, copy in late_rows:
         when_started(dr, 0, copy.wait_send)
+    for (dr, dc), copy in late_corners:
+        when_started(dr, dc, copy.wait_send)
     for dc in (1, -1):
         for chunk in range(4):
             when_started(0, dc, late_side(chunk, dc).wait_send)
@@ -661,6 +798,10 @@
 
     for chunk in range(4):
         store(chunk).wait()
+
+
+def hand_over(source, target):
+    target[...] = source[...]
 
 
 def solution(mesh):
@@ -687,8 +828,11 @@
                 pltpu.VMEM((64, 128), BF),
                 pltpu.VMEM((3, 96, 128), BF),
                 pltpu.VMEM((96, 192, 128), BF),
-                pltpu.VMEM((64, 64, 128), BF),
                 pltpu.VMEM((96, 64, 128), BF),
+                pltpu.VMEM((2, 16, 64, 128), BF),
+                pltpu.VMEM((2, 4, 64, 128), BF),
+                pltpu.VMEM((2, 4, 64, 128), BF),
+                pltpu.VMEM((2, 32, 192, 128), BF),
                 pltpu.VMEM((2, 8, 64, 128), BF),
                 pltpu.VMEM((2, 8, 64, 128), BF),
                 pltpu.VMEM((64, 64, 128), F32),
@@ -706,6 +850,11 @@
                 pltpu.VMEM((10, 8, 72, 128), F32),
                 pltpu.VMEM((10, 8, 8, 128), F32),
                 pltpu.VMEM((192, 192), BF),
+                pltpu.VMEM((2, 64, 192), BF),
+                pltpu.VMEM((1024, 256), BF),
+                pltpu.VMEM((2, 8, 256, 256), BF),
+                pltpu.VMEM((8, 128, 128), BF),
+                pltpu.VMEM((256, 256), BF),
                 pltpu.VMEM((72, 512), BF),
                 pltpu.VMEM((16, 512), BF),
                 pltpu.VMEM((64, 64, 128), BF),
@@ -717,8 +866,8 @@
                 dma((8,)),
                 dma((9,)),
                 dma((9,)),
-                dma((16,)),
-                dma((16,)),
+                dma((20,)),
+                dma((20,)),
             ],
             compiler_params=pltpu.CompilerParams(
                 collective_id=0, has_side_effects=True, vmem_limit_bytes=64 * 2**20
@@ -731,6 +880,14 @@
             conv_weights.reshape(2, 576, 64),
             coupling.reshape(2, 64),
         )
+        result = pl.pallas_call(
+            hand_over,
+            out_shape=jax.ShapeDtypeStruct((64, 64, 128), BF),
+            grid=(4,),
+            in_specs=[pl.BlockSpec((16, 64, 128), lambda i: (i, 0, 0))],
+            out_specs=pl.BlockSpec((16, 64, 128), lambda i: (i, 0, 0)),
+            compiler_params=pltpu.CompilerParams(vmem_limit_bytes=64 * 2**20),
+        )(result)
         return result[None]
 
     return jax.shard_map(

time: 53.7 us -> 55.1 us (1.026)
  Pallas kernels: 51.3 us -> 54.9 us
  local copies, waits for them, and re-layouts: 2.26 us -> 0 us
    pallas_call x0 -> x1, Pallas kernels: none -> 3.37 us  [on_device(): pl.pallas_call(hand_over, out_shape=jax.ShapeDtypeStruct((64, 64, 128), B...]
    unnamed x1 -> x0, local copies, waits for them, and re-layouts: 2.26 us -> none
where the time goes in v4:
time: 55.1 us; the launch traced here: 54.9 us
  Pallas kernels  54.9 us (100%)
    pallas_call x1, Pallas kernels, on_device(): pl.pallas_call(functools.partial(kernel, shape), out_shape=jax.ShapeDtype...  51.5 us
    pallas_call x1, Pallas kernels, on_device(): pl.pallas_call(hand_over, out_shape=jax.ShapeDtypeStruct((64, 64, 128), B...  3.37 us

profile of v4, /device:TPU:1, one launch (start us, length us, event | category | flops | bytes accessed | tf_op | source)
XLA Modules:
  0.0 54.9 jit_solution(17167261666615691553)
XLA Ops:
  0.0 51.5 %shard_map.64.source = bf16[64,64,128]{2,1,0:T(8,128)(2,1)} custom-call(s32[2]{0:T(128)} %dil.1, bf16[2,64,64,128]{3,2,1,0:T(8,128)(2,1)} %bitcast.6, bf16[64,128]{1,0:T(8,128)(2,1)} %bitcast.9, s32[64,128]{1,0:T(8,128)} %bitcast.8, bf16[2,576,64]{2,1,0:T(8,128)(2,1)} %bitcast.7, bf16[2,64]{1,0:T(2,128)(2,1)} %bitcast.10), custom_call_target="tpu_custom_call" | custom-call | tf_op jit(solution)/shard_map/pallas_call | solution.py:814
  51.5 3.4 %shard_map.65 = bf16[64,64,128]{2,1,0:T(8,128)(2,1)} custom-call(bf16[64,64,128]{2,1,0:T(8,128)(2,1)} %shard_map.64.source), custom_call_target="tpu_custom_call" | custom-call | tf_op jit(solution)/shard_map/pallas_call | solution.py:883

commit v5 on v4

--- a/solution.py
+++ b/solution.py
@@ -367,12 +367,7 @@
     heads = lax.dot_general(
         c1rows.astype(BF), w[0], NT, preferred_element_type=F32
     )
-    for b in range(3):
-        w0o[pl.ds(b * chans, chans), :] = turned(
-            jnp.concatenate([tap(3 * a + b) for a in range(3)], axis=0)
-        )
-
-    for layer, d in ((1, d1), (0, d0)):
+    def make_shifts(layer, d):
         right = n_wide + d
         left = w_wide - d
         for i in range(8):
@@ -384,33 +379,42 @@
                     jnp.where(left >= 0, left, cols + ((left + 16 * i + cols) % cols)),
                 ),
             )
-    for i in range(8):
-        umat[i] = picks(
-            cols,
+    make_shifts(1, d1)
+
+    def prepare_last():
+        for b in range(3):
+            w0o[pl.ds(b * chans, chans), :] = turned(
+                jnp.concatenate([tap(3 * a + b) for a in range(3)], axis=0)
+            )
+
+        make_shifts(0, d0)
+        for i in range(8):
+            umat[i] = picks(
+                cols,
+                jnp.where(
+                    n_one < DMAX,
+                    n_one + 16 * i,
+                    jnp.where(n_one >= cols - DMAX, (n_one + 16 * i) % cols, -1),
+                ),
+            )
+        omat[...] = picks(
+            2 * cols,
             jnp.where(
-                n_one < DMAX,
-                n_one + 16 * i,
-                jnp.where(n_one >= cols - DMAX, (n_one + 16 * i) % cols, -1),
+                n_wide < cols,
+                jnp.where(w_wide + d0 < cols, w_wide + d0, -1),
+                jnp.where(w_wide >= cols - d0, w_wide + d0 - cols, -1),
             ),
-        )
-    omat[...] = picks(
-        2 * cols,
-        jnp.where(
-            n_wide < cols,
-            jnp.where(w_wide + d0 < cols, w_wide + d0, -1),
-            jnp.where(w_wide >= cols - d0, w_wide + d0 - cols, -1),
-        ),
-        jnp.where(
-            n_wide < cols,
-            jnp.where(w_wide >= d0, cols + w_wide - d0, -1),
-            jnp.where(w_wide < d0, 2 * cols + w_wide - d0, -1),
-        ),
-    )
-    w0r[0] = turned(w[0, pl.ds(6 * chans, 3 * chans), :])
-    w0r[1] = turned(w[0, pl.ds(0, 3 * chans), :])
-    for side in (0, 1):
-        m0_e[pl.ds(side * (DMAX + rows), DMAX)] = jnp.zeros((DMAX, chans, cols), BF)
-        outside[side, pl.ds(16 - 16 * side, 16)] = jnp.zeros((DMAX, 3 * chans, cols), BF)
+            jnp.where(
+                n_wide < cols,
+                jnp.where(w_wide >= d0, cols + w_wide - d0, -1),
+                jnp.where(w_wide < d0, 2 * cols + w_wide - d0, -1),
+            ),
+        )
+        w0r[0] = turned(w[0, pl.ds(6 * chans, 3 * chans), :])
+        w0r[1] = turned(w[0, pl.ds(0, 3 * chans), :])
+        for side in (0, 1):
+            m0_e[pl.ds(side * (DMAX + rows), DMAX)] = jnp.zeros((DMAX, chans, cols), BF)
+            outside[side, pl.ds(16 - 16 * side, 16)] = jnp.zeros((DMAX, 3 * chans, cols), BF)
 
     def spread(value):
         return jnp.where(diag, jnp.concatenate([value] * 8, axis=1), 0.0)
@@ -453,7 +457,8 @@
 
     loads[5].wait()
 
-    middle = (level > 0) & (level + 1 < n_level)
+    middle = (level > 0) & (level + 2 < n_level)
+    direct = level + 2 >= n_level
 
     @pl.when(middle)
     def _():
@@ -510,6 +515,10 @@
             dst = in_corner.at[(1 - dc) // 2, (1 - dr) // 2]
         q_copies.append(((dr, dc), remote(src, dst, q_send.at[k], q_recv.at[k], peer(dr, dc, -1))))
 
+    @pl.when(level + 1 < n_level)
+    def _():
+        prepare_last()
+
     for (dr, dc), copy in q_copies:
 
         @pl.when(exists(-dr, -dc) & (level + 1 < n_level))
@@ -609,7 +618,7 @@
             found = piece if found is None else found + piece
         return found
 
-    @pl.when(level + 1 == n_level)
+    @pl.when(direct)
     def _():
         @pl.loop(0, 4)
         def _(chunk):
@@ -656,7 +665,11 @@
         for (dr, dc), copy in q_copies:
             when_started(dr, dc, copy.start)
 
-    @pl.when(level + 1 < n_level)
+    @pl.when(level + 1 == n_level)
+    def _():
+        prepare_last()
+
+    @pl.when(level + 2 < n_level)
     def _():
         @pl.loop(0, 4)
         def _(step):
@@ -670,7 +683,7 @@
             def _():
                 send_outer(1)
 
-    @pl.when(level + 1 == n_level)
+    @pl.when(direct)
     def _():
         send_outer(-1)
         send_outer(1)
@@ -798,10 +811,6 @@
 
     for chunk in range(4):
         store(chunk).wait()
-
-
-def hand_over(source, target):
-    target[...] = source[...]
 
 
 def solution(mesh):
@@ -880,14 +889,6 @@
             conv_weights.reshape(2, 576, 64),
             coupling.reshape(2, 64),
         )
-        result = pl.pallas_call(
-            hand_over,
-            out_shape=jax.ShapeDtypeStruct((64, 64, 128), BF),
-            grid=(4,),
-            in_specs=[pl.BlockSpec((16, 64, 128), lambda i: (i, 0, 0))],
-            out_specs=pl.BlockSpec((16, 64, 128), lambda i: (i, 0, 0)),
-            compiler_params=pltpu.CompilerParams(vmem_limit_bytes=64 * 2**20),
-        )(result)
         return result[None]
 
     return jax.shard_map(

time: 55.1 us -> 55.5 us (level)
  local copies, waits for them, and re-layouts: 0 us -> 2.26 us
  Pallas kernels: 54.9 us -> 53.1 us
    pallas_call x1 -> x0, Pallas kernels: 3.37 us -> none  [on_device(): pl.pallas_call(hand_over, out_shape=jax.ShapeDtypeStruct((64, 64, 128), B...]
    unnamed x0 -> x1, local copies, waits for them, and re-layouts: none -> 2.26 us
    pallas_call x1, Pallas kernels: 51.5 us -> 53.1 us  [on_device(): pl.pallas_call(functools.partial(kernel, shape), out_shape=jax.ShapeDtype...]
where the time goes in v5:
time: 55.5 us; the launch traced here: 55.4 us
  Pallas kernels  53.1 us (96%)
  local copies, waits for them, and re-layouts  2.26 us (4%)
    pallas_call x1, Pallas kernels, on_device(): pl.pallas_call(functools.partial(kernel, shape), out_shape=jax.ShapeDtype...  53.1 us
    unnamed x1, local copies, waits for them, and re-layouts  2.26 us

profile of v5, /device:TPU:1, one launch (start us, length us, event | category | flops | bytes accessed | tf_op | source)
XLA Modules:
  0.0 55.4 jit_solution(4570428858963587604)
XLA Ops:
  0.0 53.1 %shard_map.64 = bf16[64,64,128]{2,1,0:T(8,128)(2,1)} custom-call(s32[2]{0:T(128)} %dil.1, bf16[2,64,64,128]{3,2,1,0:T(8,128)(2,1)} %bitcast.7, bf16[64,128]{1,0:T(8,128)(2,1)} %bitcast.10, s32[64,128]{1,0:T(8,128)} %bitcast.9, bf16[2,576,64]{2,1,0:T(8,128)(2,1)} %bitcast.8, bf16[2,64]{1,0:T(2,128)(2,1)} %bitcast.11), custom_call_target="tpu_custom_call" | custom-call | tf_op jit(solution)/shard_map/pallas_call | solution.py:823
  53.1 2.3 %copy.8 = bf16[1,64,64,128]{3,2,1,0:T(8,128)(2,1)} copy(bf16[1,64,64,128]{3,2,1,0:T(8,128)(2,1)} %bitcast.6) | data formatting | bytes 2097152
